TPU v7x, 32 devices: a whole 2x2x4 slice. The times are simulated.
32 devices in a mesh: seq: 16 (over z, y, core), head: 2 (over x).
Axes of the slice: x: 2, y: 2, z: 4, core: 2. Of those that a mesh axis runs over, the one named last changes fastest.
Arguments:
- embedded: bfloat16 [4096, 1536], P('seq', 'head'), may hold values from -27 to 27
- grad_out: bfloat16 [4096, 1536], P('seq', 'head'), may hold values from -6 to 6
- mask_pos: int32 [608], P('seq'), may hold values from 0 to 4095, as said below
- timestep: int32 [1], replicated, may hold values from 0 to 999
- time_table: bfloat16 [1000, 1536], replicated, may hold values from -3 to 3
- mask_embed: bfloat16 [1536], replicated, may hold values from -6 to 6
- w_query: bfloat16 [1536, 768], P(None, 'head'), may hold values from -0.15625 to 0.15625
- w_key: bfloat16 [1536, 768], P(None, 'head'), may hold values from -0.15625 to 0.15625
- w_value: bfloat16 [1536, 768], P(None, 'head'), may hold values from -0.15625 to 0.15625
- w_out: bfloat16 [768, 1536], P('head'), may hold values from -0.21875 to 0.21875
Outputs:
- input_grad: bfloat16 [4096, 1536], P('seq', 'head')
- query_weight_grad: float32 [1536, 768], P('seq', 'head')
- key_weight_grad: float32 [1536, 768], P('seq', 'head')
- value_weight_grad: float32 [1536, 768], P('seq', 'head')
- out_weight_grad: float32 [1536, 768], P('seq', 'head')
Inputs may be any that keep to these rules, and one draw needn't show every extreme that they name: `mask_pos`: the entries are distinct; entries b * 38 to (b + 1) * 38 - 1 lie in positions b * 256 to (b + 1) * 256 - 1.
All inputs are finite; a program needn't handle non-finite values.
Results may differ from a plain program's by a relative error of at most 0.01.
The roundings to bfloat16 on the way count: a program that leaves them out, or rounds other values in their place, can miss the bound.
Values may be sent and summed in bfloat16 or wider, within the bound.
A program may use at most 128 MiB of HBM per device.

v0:
```python
import functools

import jax
import jax.numpy as jnp
from jax import lax
from jax.experimental import pallas as pl
from jax.experimental.pallas import tpu as pltpu
from jax.sharding import PartitionSpec as P

HEAD_DIM = 64
HALF = 1024


NEG_FILL = -1e30


def contract_first(left, right):
    return lax.dot_general(
        left, right, (((0,), (0,)), ((), ())), preferred_element_type=jnp.float32
    )


def contract_last(left, right):
    return lax.dot_general(
        left, right, (((1,), (1,)), ((), ())), preferred_element_type=jnp.float32
    )


def contract_mixed(left, right):
    return lax.dot_general(
        left, right, (((0,), (1,)), ((), ())), preferred_element_type=jnp.float32
    )


def swapped(value, axis, bit):
    count = lax.axis_size(axis)
    return lax.ppermute(value, axis, [(source, source ^ bit) for source in range(count)])


def passed_along(value, axis, steps):
    count = lax.axis_size(axis)
    first, last = (max(0, -steps), min(count, count - steps))
    return lax.ppermute(value, axis, [(source, source + steps) for source in range(first, last)])


def picked(array, index, axis):
    return lax.dynamic_index_in_dim(array, index, axis, keepdims=False)


def joined_heads(mine, head_index):
    other = swapped(mine, "head", 1)
    first = jnp.where(head_index == 0, mine, other)
    second = jnp.where(head_index == 0, other, mine)
    return jnp.concatenate([first, second], axis=1)


def core_summed(parts, seq_index):
    count = lax.axis_size("seq")
    core = seq_index % 2
    blocks = [part.reshape(count // 4, 2, 2, -1, part.shape[1]) for part in parts]
    kept = jnp.concatenate([picked(block, core, 2) for block in blocks], axis=3)
    sent = jnp.concatenate([picked(block, 1 - core, 2) for block in blocks], axis=3)
    return kept + swapped(sent, "seq", 1)


def side_summed(blocks, seq_index):
    side = seq_index // 2 % 2
    sent = picked(blocks, 1 - side, 1).astype(jnp.bfloat16)
    return picked(blocks, side, 1) + swapped(sent, "seq", 2).astype(jnp.float32)


def group_summed(blocks):
    groups, rows, width = blocks.shape
    members = [[g * 4 + place for g in range(groups)] for place in range(4)]
    return lax.psum_scatter(
        blocks.reshape(groups * rows, width),
        "seq",
        scatter_dimension=0,
        axis_index_groups=members,
        tiled=True,
    )


def closing_kernel(
    groups,
    early_ref,
    late_ref,
    kept_ref,
    sent_ref,
    early_out,
    late_out,
    summed_out,
    early_send,
    early_slots,
    core_slot,
    side_send,
    side_slot,
    total,
    late_send,
    late_slots,
    head_slot,
    single_send,
    single_recv,
    early_send_sems,
    early_recv_sems,
    late_send_sems,
    late_recv_sems,
):
    me = lax.axis_index("seq")
    head = lax.axis_index("head")
    core = lax.rem(me, 2)
    side = lax.rem(me // 2, 2)
    group = me // 4
    place = lax.rem(me, 4)
    core_peer = me + 1 - 2 * core
    side_peer = me + 2 - 4 * side
    targets = [lax.rem(group + step, groups) for step in range(1, groups)]
    peers = [(core_peer, head), (side_peer, head), (me, 1 - head)]
    peers += [(target * 4 + place, head) for target in targets]

    barrier = pltpu.get_barrier_semaphore()
    for peer in peers:
        pl.semaphore_signal(barrier, inc=1, device_id=peer, device_id_type=pl.DeviceIdType.MESH)
    pl.semaphore_wait(barrier, len(peers))

    def remote(source, target, send, recv, peer):
        copy = pltpu.make_async_remote_copy(
            src_ref=source,
            dst_ref=target,
            send_sem=send,
            recv_sem=recv,
            device_id=peer,
            device_id_type=pl.DeviceIdType.MESH,
        )
        copy.start()
        return copy

    core_copy = remote(
        late_ref.at[1 - core], core_slot, single_send.at[0], single_recv.at[0], peers[0]
    )
    early_send[...] = early_ref[...].astype(jnp.bfloat16)
    early_copies = []
    for step in range(1, groups):
        early_copies.append(
            remote(
                early_send.at[targets[step - 1]],
                early_slots.at[step - 1],
                early_send_sems.at[step - 1],
                early_recv_sems.at[step - 1],
                peers[2 + step],
            )
        )
    head_copy = remote(sent_ref, head_slot, single_send.at[2], single_recv.at[2], peers[2])
    core_copy.wait()
    side_send[...] = (late_ref[core, 1 - side] + core_slot[1 - side]).astype(jnp.bfloat16)
    side_copy = remote(side_send, side_slot, single_send.at[1], single_recv.at[1], peers[1])
    total[...] = late_ref[core, side] + core_slot[side]
    side_copy.wait()
    total[...] = total[...] + side_slot[...].astype(jnp.float32)
    late_send[...] = total[...].astype(jnp.bfloat16)
    late_copies = []
    for step in range(1, groups):
        late_copies.append(
            remote(
                late_send.at[targets[step - 1]],
                late_slots.at[step - 1],
                late_send_sems.at[step - 1],
                late_recv_sems.at[step - 1],
                peers[2 + step],
            )
        )
    head_copy.wait()
    summed_out[...] = kept_ref[...] + head_slot[...]
    result = early_ref[group]
    for step in range(1, groups):
        early_copies[step - 1].wait()
        result = result + early_slots[step - 1].astype(jnp.float32)
    early_out[...] = result
    result = total[group]
    for step in range(1, groups):
        late_copies[step - 1].wait()
        result = result + late_slots[step - 1].astype(jnp.float32)
    late_out[...] = result


def closing_sums(early, late, kept, sent):
    groups, rows, width = early.shape
    chunk = (groups, rows, width)
    slots = (groups - 1, rows, width)
    return pl.pallas_call(
        functools.partial(closing_kernel, groups),
        out_shape=(
            jax.ShapeDtypeStruct((rows, width), jnp.float32),
            jax.ShapeDtypeStruct((rows, width), jnp.float32),
            jax.ShapeDtypeStruct(kept.shape, jnp.float32),
        ),
        in_specs=[pl.BlockSpec(memory_space=pltpu.VMEM)] * 4,
        out_specs=[pl.BlockSpec(memory_space=pltpu.VMEM)] * 3,
        scratch_shapes=[
            pltpu.VMEM(chunk, jnp.bfloat16),
            pltpu.VMEM(slots, jnp.bfloat16),
            pltpu.VMEM((2,) + chunk, jnp.float32),
            pltpu.VMEM(chunk, jnp.bfloat16),
            pltpu.VMEM(chunk, jnp.bfloat16),
            pltpu.VMEM(chunk, jnp.float32),
            pltpu.VMEM(chunk, jnp.bfloat16),
            pltpu.VMEM(slots, jnp.bfloat16),
            pltpu.VMEM(kept.shape, jnp.float32),
            pltpu.SemaphoreType.DMA((3,)),
            pltpu.SemaphoreType.DMA((3,)),
            pltpu.SemaphoreType.DMA((groups - 1,)),
            pltpu.SemaphoreType.DMA((groups - 1,)),
            pltpu.SemaphoreType.DMA((groups - 1,)),
            pltpu.SemaphoreType.DMA((groups - 1,)),
        ],
        compiler_params=pltpu.CompilerParams(
            collective_id=0, has_side_effects=True, vmem_limit_bytes=48 * 1024 * 1024
        ),
    )(early, late, kept, sent)


def body(
    embedded, grad_out, mask_pos, timestep, time_table, mask_embed, w_query, w_key, w_value, w_out
):
    seq_index = lax.axis_index("seq")
    seq_count = lax.axis_size("seq")
    head_place = lax.axis_index("head")
    core, side = seq_index % 2, seq_index // 2 % 2
    slab_rows = embedded.shape[0]
    total_len = slab_rows * seq_count
    scale = HEAD_DIM ** (-0.5)
    full_rows = joined_heads(embedded, head_place)
    full_grad = joined_heads(grad_out, head_place)
    positions = seq_index * slab_rows + jnp.arange(slab_rows, dtype=jnp.int32)
    masked = jnp.any(positions[:, None] == mask_pos[None, :], axis=1)
    time_row = lax.dynamic_slice_in_dim(time_table, timestep[0], 1, 0).astype(jnp.float32)
    hidden = (
        jnp.where(
            masked[:, None], mask_embed.astype(jnp.float32)[None, :], full_rows.astype(jnp.float32)
        )
        + time_row
    ).astype(jnp.bfloat16)
    key_rows = jnp.dot(hidden, w_key, preferred_element_type=jnp.float32).astype(jnp.bfloat16)
    value_rows = jnp.dot(hidden, w_value, preferred_element_type=jnp.float32).astype(jnp.bfloat16)
    queries = jnp.dot(hidden, w_query, preferred_element_type=jnp.float32).astype(jnp.bfloat16)
    grad_attn = contract_last(full_grad, w_out).astype(jnp.bfloat16)
    group_width = queries.shape[1]
    head_count = group_width // HEAD_DIM

    own = jnp.concatenate([key_rows, value_rows], axis=1)
    below = passed_along(own, "seq", 4)
    above = passed_along(own, "seq", -4)
    plane_side = swapped(own, "seq", 2)
    plane_core = swapped(own, "seq", 1)
    far_side = swapped(jnp.where(side == 1, below, above), "seq", 2)
    far_core = swapped(jnp.where(core == 1, below, above), "seq", 1)
    plane_both = swapped(plane_side, "seq", 1)
    far_both = swapped(far_side, "seq", 1)
    slabs = jnp.concatenate(
        [far_both, plane_both, far_core, plane_core, far_side, plane_side, own, below, above],
        axis=0,
    )
    core_step = 4 - 8 * (1 - core)
    side_step = 4 - 8 * (1 - side)
    numbers = [
        (seq_index ^ 3) + side_step,
        seq_index ^ 3,
        (seq_index ^ 1) + core_step,
        seq_index ^ 1,
        (seq_index ^ 2) + side_step,
        seq_index ^ 2,
        seq_index,
        seq_index - 4,
        seq_index + 4,
    ]
    offsets = jnp.arange(slab_rows, dtype=jnp.int32)
    key_pos = jnp.concatenate([number * slab_rows + offsets for number in numbers])
    keys_all = slabs[:, :group_width]
    values_all = slabs[:, group_width:]
    distance_grid = positions[:, None] - key_pos[None, :]
    band = (
        (jnp.abs(distance_grid) <= HALF) & (key_pos[None, :] >= 0) & (key_pos[None, :] < total_len)
    )
    head_outputs = []
    query_grads = []
    key_grads = []
    value_grads = []
    for head_index in range(head_count):
        lower_col = head_index * HEAD_DIM
        upper_col = lower_col + HEAD_DIM
        head_query = queries[:, lower_col:upper_col]
        head_keys = keys_all[:, lower_col:upper_col]
        head_values = values_all[:, lower_col:upper_col]
        head_grad = grad_attn[:, lower_col:upper_col]
        scores = contract_last(head_query, head_keys) * scale
        scores = jnp.where(band, scores, NEG_FILL)
        row_max = jnp.max(scores, axis=1, keepdims=True)
        log_total = row_max + jnp.log(jnp.sum(jnp.exp(scores - row_max), axis=1, keepdims=True))
        attention = jnp.exp(scores - log_total)
        rounded = attention.astype(jnp.bfloat16)
        output = jnp.dot(rounded, head_values, preferred_element_type=jnp.float32).astype(
            jnp.bfloat16
        )
        head_outputs.append(output)
        delta = jnp.sum(head_grad.astype(jnp.float32) * output.astype(jnp.float32), axis=1)
        dprob = contract_last(head_grad, head_values)
        dscore = (attention * (dprob - delta[:, None])).astype(jnp.bfloat16)
        query_grads.append(scale * jnp.dot(dscore, head_keys, preferred_element_type=jnp.float32))
        key_grads.append(scale * contract_first(head_query, dscore))
        value_grads.append(contract_first(head_grad, rounded))
    attn_out = jnp.concatenate(head_outputs, axis=1)
    query_rounded = jnp.concatenate(query_grads, axis=1).astype(jnp.bfloat16)
    slab_grads = jnp.concatenate(key_grads + value_grads, axis=0)

    def slab_of(first, count):
        return slab_grads[:, first * slab_rows : (first + count) * slab_rows]

    by_core = swapped(slab_of(0, 4), "seq", 1)
    for_side = (by_core[:, : 2 * slab_rows] + slab_of(4, 2)).astype(jnp.bfloat16)
    early_part = core_summed(
        [contract_first(hidden, query_rounded), contract_first(full_grad, attn_out)], seq_index
    )
    by_side, early_part = lax.optimization_barrier((swapped(for_side, "seq", 2), early_part))
    by_side = by_side.astype(jnp.float32)
    early_part = side_summed(early_part, seq_index)
    core_far, core_own = by_core[:, 2 * slab_rows : 3 * slab_rows], by_core[:, 3 * slab_rows :]
    side_far, side_own = by_side[:, :slab_rows], by_side[:, slab_rows:]
    to_below = slab_of(7, 1) + jnp.where(core == 1, core_far, 0.0) + jnp.where(side == 1, side_far, 0.0)
    to_above = slab_of(8, 1) + jnp.where(core == 0, core_far, 0.0) + jnp.where(side == 0, side_far, 0.0)
    slab_total = slab_of(6, 1) + core_own + side_own
    slab_total = slab_total + passed_along(to_below.astype(jnp.bfloat16), "seq", -4).astype(jnp.float32)
    slab_total = slab_total + passed_along(to_above.astype(jnp.bfloat16), "seq", 4).astype(jnp.float32)
    pair_rounded = slab_total.astype(jnp.bfloat16)

    partial_grad = contract_last(query_rounded, w_query)
    partial_grad = partial_grad + contract_mixed(pair_rounded[:group_width], w_key)
    partial_grad = partial_grad + contract_mixed(pair_rounded[group_width:], w_value)
    half = embedded.shape[1]
    left, right = partial_grad[:, :half], partial_grad[:, half:]
    kept = jnp.where(head_place == 0, left, right)
    sent = jnp.where(head_place == 0, right, left)
    late_part = lax.dot_general(
        hidden, pair_rounded, (((0,), (1,)), ((), ())), preferred_element_type=jnp.float32
    )
    groups = seq_count // 4
    if groups > 4:
        early = group_summed(early_part)
        late = group_summed(side_summed(core_summed([late_part], seq_index), seq_index))
        summed = kept + swapped(sent, "head", 1)
    else:
        rows = late_part.shape[0] // seq_count
        blocks = late_part.reshape(groups, 2, 2, rows, late_part.shape[1]).transpose(2, 1, 0, 3, 4)
        early, late, summed = closing_sums(early_part, blocks, kept, sent)
    input_grad = jnp.where(masked[:, None], 0.0, summed).astype(jnp.bfloat16)
    return (
        input_grad,
        early[:, :group_width],
        late[:, :group_width],
        late[:, group_width:],
        early[:, group_width:],
    )


def solution(mesh):
    placed = (
        P("seq", "head"),
        P("seq", "head"),
        P("seq"),
        P(),
        P(),
        P(),
        P(None, "head"),
        P(None, "head"),
        P(None, "head"),
        P("head", None),
    )
    return jax.shard_map(
        body,
        mesh=mesh,
        in_specs=placed,
        out_specs=(
            P("seq", "head"),
            P("seq", "head"),
            P("seq", "head"),
            P("seq", "head"),
            P("seq", "head"),
        ),
        check_vma=False,
    )
```

profile of v0, /device:TPU:0, one launch (start us, length us, event | category | flops | bytes accessed | tf_op | source)
XLA Modules:
  0.0 173.7 jit_solution(8889829748792623723)
XLA Ops:
  0.6 3.0 %collective-permute-start = (bf16[256,768]{1,0:T(8,128)(2,1)}, bf16[256,768]{1,0:T(8,128)(2,1)S(1)}, u32[]{:S(2)}, u32[]{:S(2)}) collective-permute-start(bf16[256,768]{1,0:T(8,128)(2,1)} %param.10), channel_id=1, source_target_pairs={{0,1},{1,0},{2,3},{3,2},{4,5},{5,4},{6,7},{7,6},{8,9},{9,8},{10,11... | collective-permute-start | bytes 1179656 | tf_op jit(solution)/shard_map/ppermute | solution.py:37
  5.1 0.8 convert_reduce_fusion
  5.9 0.7 compare_reduce_fusion
  6.7 7.1 %collective-permute-done = bf16[256,768]{1,0:T(8,128)(2,1)S(1)} collective-permute-done((bf16[256,768]{1,0:T(8,128)(2,1)}, bf16[256,768]{1,0:T(8,128)(2,1)S(1)}, u32[]{:S(2)}, u32[]{:S(2)}) %collective-permute-start) | collective-permute-done | bytes 393248 | tf_op jit(solution)/shard_map/ppermute | solution.py:37
  13.8 1.1 broadcast_select_fusion.5
  14.9 2.2 %convolution_convert_fusion.2 = bf16[256,384]{1,0:T(8,128)(2,1)S(1)} fusion(bf16[1536,384]{1,0:T(8,128)(2,1)} %param.17, bf16[256,768]{1,0:T(8,128)(2,1)S(1)} %get-tuple-element.34, bf16[256,768]{1,0:T(8,128)(2,1)S(1)} %get-tuple-element.33, f32[1536]{0:T(1024)S(1)} %convert_reduce_fusion, f32[1536]{0:T(1024)S(1)} %convert_element_type.146, ...), kind=kOutput, calls=%fused_computation.85 | convolution fusion | flops 304840704 | bytes 2175232 | tf_op jit(solution)/shard_map/dot_general | solution.py:243
  17.8 4.1 %collective-permute-start.1 = (bf16[256,768]{1,0:T(8,128)(2,1)S(1)}, bf16[256,768]{1,0:T(8,128)(2,1)S(1)}, u32[]{:S(2)}, u32[]{:S(2)}) collective-permute-start(bf16[256,768]{1,0:T(8,128)(2,1)S(1)} %pad_maximum_fusion.4), channel_id=1, source_target_pairs={{0,8},{2,10},{4,12},{6,14},{8,16},{10,18},{12,20},{14,22},{16,24},... | collective-permute-start | bytes 1179656 | tf_op jit(solution)/shard_map/ppermute | solution.py:43
  21.9 1.3 collective-permute-start.2
  23.2 1.6 collective-permute-start.5
  24.8 3.4 %collective-permute-done.1 = bf16[256,768]{1,0:T(8,128)(2,1)S(1)} collective-permute-done((bf16[256,768]{1,0:T(8,128)(2,1)S(1)}, bf16[256,768]{1,0:T(8,128)(2,1)S(1)}, u32[]{:S(2)}, u32[]{:S(2)}) %collective-permute-start.1) | collective-permute-done | bytes 393248 | tf_op jit(solution)/shard_map/ppermute | solution.py:43
  28.2 4.1 %collective-permute-done.2 = bf16[256,768]{1,0:T(8,128)(2,1)S(1)} collective-permute-done((bf16[256,768]{1,0:T(8,128)(2,1)S(1)}, bf16[256,768]{1,0:T(8,128)(2,1)S(1)}, u32[]{:S(2)}, u32[]{:S(2)}) %collective-permute-start.2) | collective-permute-done | bytes 393248 | tf_op jit(solution)/shard_map/ppermute | solution.py:43
  32.4 1.6 collective-permute-start.3
  34.7 5.6 %collective-permute-done.3 = bf16[256,768]{1,0:T(8,128)(2,1)S(1)} collective-permute-done((bf16[256,768]{1,0:T(8,128)(2,1)S(1)}, bf16[256,768]{1,0:T(8,128)(2,1)S(1)}, u32[]{:S(2)}, u32[]{:S(2)}) %collective-permute-start.3) | collective-permute-done | bytes 393248 | tf_op jit(solution)/shard_map/ppermute | solution.py:37
  43.1 1.3 fusion.122
  44.4 1.2 fusion.127
  45.6 1.3 fusion.126
  46.9 1.2 fusion.125
  48.0 1.3 fusion.124
  49.3 1.2 fusion.123
  53.7 0.8 convolution_convert_fusion.7
  56.8 1.5 multiply_reduce_fusion
  59.8 0.8 fusion.13
  61.2 0.8 fusion.15
  62.6 0.8 fusion.17
  63.3 0.8 fusion.36
  70.0 2.5 %slice.206 = f32[768,1024]{1,0:T(8,128)} slice(f32[768,2304]{1,0:T(8,128)S(1)} %convolution_dynamic-update-slice_fusion), slice={[0:768], [0:1024]} | slice | bytes 6291456 | tf_op jit(solution)/shard_map/slice | solution.py:316
  72.8 1.0 fusion.40
  74.5 1.8 %concatenate.46 = bf16[256,384]{1,0:T(8,128)(2,1)} concatenate(bf16[256,64]{1,0:T(8,128)(2,1)} %copy-done.24, bf16[256,64]{1,0:T(8,128)(2,1)} %copy-done.23, bf16[256,64]{1,0:T(8,128)(2,1)} %copy-done.22, bf16[256,64]{1,0:T(8,128)(2,1)} %copy-done.21, bf16[256,64]{1,0:T(8,128)(2,1)} %copy-done.20, bf16[256,64]{1,0:T(8,128)(2,1)} %get-tuple-element.53), dimensions={1} | concatenate | bytes 393216 | tf_op jit(solution)/shard_map/concatenate | solution.py:311
  76.3 2.3 %fusion.42 = bf16[256,384]{0,1:T(8,128)(2,1)} fusion(bf16[256,384]{0,1:T(8,128)(2,1)} %copy-done.16, bf16[256,2304]{1,0:T(8,128)(2,1)S(1)} %fusion.16, bf16[2304,768]{1,0:T(8,128)(2,1)} %copy-done.1), kind=kOutput, calls=%fused_computation.108 | convolution fusion | flops 75530240 | bytes 1802240 | tf_op jit(solution)/shard_map/dot_general | solution.py:308
  78.6 2.5 %fusion.44 = bf16[256,384]{0,1:T(8,128)(2,1)} fusion(bf16[256,384]{0,1:T(8,128)(2,1)} %fusion.42, bf16[256,2304]{1,0:T(8,128)(2,1)S(1)} %fusion.17, bf16[2304,768]{1,0:T(8,128)(2,1)} %copy-done.1), kind=kOutput, calls=%fused_computation.110 | convolution fusion | flops 75530240 | bytes 1802240 | tf_op jit(solution)/shard_map/dot_general | solution.py:308
  83.3 1.6 pad_maximum_fusion
  85.2 3.0 %fusion.32 = bf16[768,512]{1,0:T(8,128)(2,1)} fusion(f32[768,2304]{1,0:T(8,128)} %copy-done.2, f32[768,1024]{1,0:T(8,128)} %collective-permute-done.10), kind=kLoop, calls=%fused_computation.75 | loop fusion | flops 786432 | bytes 3932160 | tf_op jit(solution)/shard_map/convert_element_type | solution.py:319
  88.2 1.5 collective-permute-start.11
  89.9 1.9 %maximum_add_fusion = f32[4,2,96,768]{3,2,0,1:T(8,128)S(1)} fusion(f32[4,2,96,768]{3,2,0,1:T(8,128)} %collective-permute-done.12, f32[4,2,96,384]{3,2,0,1:T(8,128)S(1)} %bitcast.53, f32[4,2,96,384]{3,2,0,1:T(8,128)S(1)} %bitcast.54), kind=kLoop, calls=%fused_computation.51 | loop fusion | flops 1179648 | bytes 7077888 | tf_op jit(solution)/shard_map/add | solution.py:63
  91.8 16.4 %collective-permute-done.11 = bf16[768,512]{1,0:T(8,128)(2,1)} collective-permute-done((bf16[768,512]{1,0:T(8,128)(2,1)}, bf16[768,512]{1,0:T(8,128)(2,1)}, u32[]{:S(2)}, u32[]{:S(2)}) %collective-permute-start.11) | collective-permute-done | bytes 786464 | tf_op jit(solution)/shard_map/ppermute | solution.py:37
  108.2 1.3 convert_element_type.187
  109.5 2.0 %fusion.48 = (bf16[768,256]{1,0:T(8,128)(2,1)S(1)}, bf16[768,256]{1,0:T(8,128)(2,1)S(1)}) fusion(f32[768,2304]{1,0:T(8,128)} %copy-done.2, f32[768,512]{1,0:T(8,128)S(1)} %convert_element_type.187, f32[768,1024]{1,0:T(8,128)} %collective-permute-done.10, pred[]{:T(512)S(6)} %eq.44, pred[]{:T(512)S(6)} %eq.45, pred[]{:T(512)S(6)} %eq.47, pred[]{:T(512)S(6)} %eq.46), kind=kLoop, calls=%fused_computation.116 | loop fusion | flops 1966080 | bytes 3932164 | tf_op jit(solution)/shard_map/convert_element_type | solution.py:331
  111.5 1.3 collective-permute-start.14
  112.8 4.9 %collective-permute-start.15 = (bf16[768,256]{1,0:T(8,128)(2,1)S(1)}, bf16[768,256]{1,0:T(8,128)(2,1)S(1)}, u32[]{:S(2)}, u32[]{:S(2)}) collective-permute-start(bf16[768,256]{1,0:T(8,128)(2,1)S(1)} %get-tuple-element.22), channel_id=1, source_target_pairs={{0,8},{2,10},{4,12},{6,14},{8,16},{10,18},{12,20},{14,22},{16,24},... | collective-permute-start | bytes 1179656 | tf_op jit(solution)/shard_map/ppermute | solution.py:43
  118.5 1.6 collective-permute-start.13
  120.0 4.4 %collective-permute-done.14 = bf16[768,256]{1,0:T(8,128)(2,1)S(1)} collective-permute-done((bf16[768,256]{1,0:T(8,128)(2,1)S(1)}, bf16[768,256]{1,0:T(8,128)(2,1)S(1)}, u32[]{:S(2)}, u32[]{:S(2)}) %collective-permute-start.14) | collective-permute-done | bytes 393248 | tf_op jit(solution)/shard_map/ppermute | solution.py:43
  124.4 1.2 collective-permute-done.15
  125.6 1.7 fusion.51
  127.3 0.9 fusion.118
  129.2 2.5 %copy.62 = f32[4,2,2,96,768]{4,3,0,1,2:T(8,128)} copy(f32[4,2,2,96,768]{4,3,2,1,0:T(8,128)S(1)} %bitcast.50) | data formatting | bytes 9437184 | tf_op jit(solution)/shard_map/reshape | solution.py:352
  133.0 38.4 %shard_map.137 = (f32[96,768]{1,0:T(8,128)S(1)}, f32[96,768]{1,0:T(8,128)S(1)}, f32[256,768]{1,0:T(8,128)S(1)}) custom-call(f32[4,96,768]{2,1,0:T(8,128)S(1)} %bitcast_add_fusion.early_ref, f32[2,2,4,96,768]{4,3,2,1,0:T(8,128)} %bitcast.49, f32[256,768]{1,0:T(8,128)S(1)} %get-tuple-element.28.kept_ref, f32[256,768]{1,0:T(8,128)S(1)} %get-tuple-element.27.sent_ref), custom_call_target="tpu_custom_call" | custom-call | tf_op jit(solution)/shard_map/pallas_call | solution.py:190
  171.4 0.9 select_convert_fusion
  172.3 0.7 fusion.120
  (151 shorter events, 26.0 us)
Async XLA Ops:
  0.6 39.7 %copy-start = (bf16[1536,384]{1,0:T(8,128)(2,1)S(1)}, bf16[1536,384]{1,0:T(8,128)(2,1)}, u32[]{:S(2)}) copy-start(bf16[1536,384]{1,0:T(8,128)(2,1)} %param.16) | copy-start | bytes 3538948
  0.6 13.2 %collective-permute-start = (bf16[256,768]{1,0:T(8,128)(2,1)}, bf16[256,768]{1,0:T(8,128)(2,1)S(1)}, u32[]{:S(2)}, u32[]{:S(2)}) collective-permute-start(bf16[256,768]{1,0:T(8,128)(2,1)} %param.10), channel_id=1, source_target_pairs={{0,1},{1,0},{2,3},{3,2},{4,5},{5,4},{6,7},{7,6},{8,9},{9,8},{10,11... | collective-permute-start | bytes 1179656 | tf_op jit(solution)/shard_map/ppermute | solution.py:37
  3.6 30.4 %collective-permute-start.9 = (bf16[256,768]{1,0:T(8,128)(2,1)}, bf16[256,768]{1,0:T(8,128)(2,1)S(1)}, u32[]{:S(2)}, u32[]{:S(2)}) collective-permute-start(bf16[256,768]{1,0:T(8,128)(2,1)} %param.11), channel_id=1, source_target_pairs={{0,1},{1,0},{2,3},{3,2},{4,5},{5,4},{6,7},{7,6},{8,9},{9,8},{10,11... | collective-permute-start | bytes 1179656 | tf_op jit(solution)/shard_map/ppermute | solution.py:37
  6.7 33.6 %copy-start.26 = (pred[256]{0:T(512)(128)(4,1)}, pred[256]{0:T(512)(128)(4,1)S(1)}, u32[]{:S(2)}) copy-start(pred[256]{0:T(512)(128)(4,1)S(1)} %compare_reduce_fusion) | copy-start | bytes 772
  14.9 25.4 %copy-start.3 = (bf16[256,768]{1,0:T(8,128)(2,1)}, bf16[256,768]{1,0:T(8,128)(2,1)S(1)}, u32[]{:S(2)}) copy-start(bf16[256,768]{1,0:T(8,128)(2,1)S(1)} %get-tuple-element.33) | copy-start | bytes 1179652
  14.9 25.4 %copy-start.6 = (bf16[256,768]{1,0:T(8,128)(2,1)}, bf16[256,768]{1,0:T(8,128)(2,1)S(1)}, u32[]{:S(2)}) copy-start(bf16[256,768]{1,0:T(8,128)(2,1)S(1)} %get-tuple-element.34) | copy-start | bytes 1179652
  14.9 2.2 %copy-start.14 = (bf16[1536,384]{1,0:T(8,128)(2,1)S(1)}, bf16[1536,384]{1,0:T(8,128)(2,1)}, u32[]{:S(2)}) copy-start(bf16[1536,384]{1,0:T(8,128)(2,1)} %param.18) | copy-start | bytes 3538948
  17.1 16.9 %copy-start.25 = (bf16[256,768]{1,0:T(8,128)(2,1)S(1)}, bf16[256,768]{1,0:T(8,128)(2,1)}, u32[]{:S(2)}) copy-start(bf16[256,768]{1,0:T(8,128)(2,1)} %param.11) | copy-start | bytes 1179652
  17.8 10.4 %collective-permute-start.1 = (bf16[256,768]{1,0:T(8,128)(2,1)S(1)}, bf16[256,768]{1,0:T(8,128)(2,1)S(1)}, u32[]{:S(2)}, u32[]{:S(2)}) collective-permute-start(bf16[256,768]{1,0:T(8,128)(2,1)S(1)} %pad_maximum_fusion.4), channel_id=1, source_target_pairs={{0,8},{2,10},{4,12},{6,14},{8,16},{10,18},{12,20},{14,22},{16,24},... | collective-permute-start | bytes 1179656 | tf_op jit(solution)/shard_map/ppermute | solution.py:43
  21.9 10.5 %collective-permute-start.2 = (bf16[256,768]{1,0:T(8,128)(2,1)S(1)}, bf16[256,768]{1,0:T(8,128)(2,1)S(1)}, u32[]{:S(2)}, u32[]{:S(2)}) collective-permute-start(bf16[256,768]{1,0:T(8,128)(2,1)S(1)} %pad_maximum_fusion.4), channel_id=1, source_target_pairs={{8,0},{10,2},{12,4},{14,6},{16,8},{18,10},{20,12},{22,14},{24,16},... | collective-permute-start | bytes 1179656 | tf_op jit(solution)/shard_map/ppermute | solution.py:43
  23.2 10.9 %collective-permute-start.5 = (bf16[256,768]{1,0:T(8,128)(2,1)S(1)}, bf16[256,768]{1,0:T(8,128)(2,1)S(1)}, u32[]{:S(2)}, u32[]{:S(2)}) collective-permute-start(bf16[256,768]{1,0:T(8,128)(2,1)S(1)} %pad_maximum_fusion.4), channel_id=1, source_target_pairs={{0,4},{2,6},{4,0},{6,2},{8,12},{10,14},{12,8},{14,10},{16,20},{18,... | collective-permute-start | bytes 1179656 | tf_op jit(solution)/shard_map/ppermute | solution.py:37
  32.4 7.9 %collective-permute-start.3 = (bf16[256,768]{1,0:T(8,128)(2,1)S(1)}, bf16[256,768]{1,0:T(8,128)(2,1)S(1)}, u32[]{:S(2)}, u32[]{:S(2)}) collective-permute-start(bf16[256,768]{1,0:T(8,128)(2,1)S(1)} %get-tuple-element.32), channel_id=1, source_target_pairs={{0,4},{2,6},{4,0},{6,2},{8,12},{10,14},{12,8},{14,10},{16,20},{18,... | collective-permute-start | bytes 1179656 | tf_op jit(solution)/shard_map/ppermute | solution.py:37
  34.0 8.9 %collective-permute-start.8 = (bf16[256,768]{1,0:T(8,128)(2,1)S(1)}, bf16[256,768]{1,0:T(8,128)(2,1)S(1)}, u32[]{:S(2)}, u32[]{:S(2)}) collective-permute-start(bf16[256,768]{1,0:T(8,128)(2,1)S(1)} %pad_maximum_fusion.4), channel_id=1, source_target_pairs={{0,2},{2,0},{4,6},{6,4},{8,10},{10,8},{12,14},{14,12},{16,18},{18,... | collective-permute-start | bytes 1179656 | tf_op jit(solution)/shard_map/ppermute | solution.py:37
  34.1 8.0 %copy-start.9 = (bf16[256,768]{1,0:T(8,128)(2,1)}, bf16[256,768]{1,0:T(8,128)(2,1)S(1)}, u32[]{:S(2)}) copy-start(bf16[256,768]{1,0:T(8,128)(2,1)S(1)} %get-tuple-element.29) | copy-start | bytes 1179652
  34.1 8.0 %copy-start.11 = (bf16[256,768]{1,0:T(8,128)(2,1)}, bf16[256,768]{1,0:T(8,128)(2,1)S(1)}, u32[]{:S(2)}) copy-start(bf16[256,768]{1,0:T(8,128)(2,1)S(1)} %get-tuple-element.30) | copy-start | bytes 1179652
  34.1 7.4 %copy-start.29 = (bf16[384,1536]{1,0:T(8,128)(2,1)S(1)}, bf16[384,1536]{1,0:T(8,128)(2,1)}, u32[]{:S(2)}) copy-start(bf16[384,1536]{1,0:T(8,128)(2,1)} %param.19) | copy-start | bytes 3538948
  34.1 8.0 %collective-permute-start.6 = (bf16[256,768]{1,0:T(8,128)(2,1)S(1)}, bf16[256,768]{1,0:T(8,128)(2,1)S(1)}, u32[]{:S(2)}, u32[]{:S(2)}) collective-permute-start(bf16[256,768]{1,0:T(8,128)(2,1)S(1)} %collective-permute-done.5), channel_id=1, source_target_pairs={{0,2},{2,0},{4,6},{6,4},{8,10},{10,8},{12,14},{14,12},{16,18},{18,... | collective-permute-start | bytes 1179656 | tf_op jit(solution)/shard_map/ppermute | solution.py:37
  40.3 1.8 %collective-permute-start.4 = (bf16[256,768]{1,0:T(8,128)(2,1)S(1)}, bf16[256,768]{1,0:T(8,128)(2,1)S(1)}, u32[]{:S(2)}, u32[]{:S(2)}) collective-permute-start(bf16[256,768]{1,0:T(8,128)(2,1)S(1)} %collective-permute-done.3), channel_id=1, source_target_pairs={{0,2},{2,0},{4,6},{6,4},{8,10},{10,8},{12,14},{14,12},{16,18},{18,... | collective-permute-start | bytes 1179656 | tf_op jit(solution)/shard_map/ppermute | solution.py:37
  41.0 1.9 %collective-permute-start.7 = (bf16[256,768]{1,0:T(8,128)(2,1)S(1)}, bf16[256,768]{1,0:T(8,128)(2,1)S(1)}, u32[]{:S(2)}, u32[]{:S(2)}) collective-permute-start(bf16[256,768]{1,0:T(8,128)(2,1)S(1)} %get-tuple-element.31), channel_id=1, source_target_pairs={{0,2},{2,0},{4,6},{6,4},{8,10},{10,8},{12,14},{14,12},{16,18},{18,... | collective-permute-start | bytes 1179656 | tf_op jit(solution)/shard_map/ppermute | solution.py:37
  43.1 29.7 %copy-start.1 = (bf16[2304,768]{1,0:T(8,128)(2,1)}, bf16[2304,768]{1,0:T(8,128)(2,1)S(1)}, u32[]{:S(2)}) copy-start(bf16[2304,768]{1,0:T(8,128)(2,1)S(1)} %constant_dynamic-update-slice_fusion.1) | copy-start | bytes 10616836
  52.1 4.7 %copy-start.20 = (bf16[256,64]{1,0:T(8,128)(2,1)}, bf16[256,64]{1,0:T(8,128)(2,1)S(1)}, u32[]{:S(2)}) copy-start(bf16[256,64]{1,0:T(8,128)(2,1)S(1)} %convolution_convert_fusion.5) | copy-start | bytes 98308
  53.2 3.5 %copy-start.21 = (bf16[256,64]{1,0:T(8,128)(2,1)}, bf16[256,64]{1,0:T(8,128)(2,1)S(1)}, u32[]{:S(2)}) copy-start(bf16[256,64]{1,0:T(8,128)(2,1)S(1)} %convolution_convert_fusion.6) | copy-start | bytes 98308
  54.5 2.3 %copy-start.22 = (bf16[256,64]{1,0:T(8,128)(2,1)}, bf16[256,64]{1,0:T(8,128)(2,1)S(1)}, u32[]{:S(2)}) copy-start(bf16[256,64]{1,0:T(8,128)(2,1)S(1)} %convolution_convert_fusion.7) | copy-start | bytes 98308
  55.7 1.1 copy-start.23
  56.8 2.1 %copy-start.24 = (bf16[256,64]{1,0:T(8,128)(2,1)}, bf16[256,64]{1,0:T(8,128)(2,1)S(1)}, u32[]{:S(2)}) copy-start(bf16[256,64]{1,0:T(8,128)(2,1)S(1)} %convolution_convert_fusion.9) | copy-start | bytes 98308
  70.0 3.9 %copy-start.2 = (f32[768,2304]{1,0:T(8,128)}, f32[768,2304]{1,0:T(8,128)S(1)}, u32[]{:S(2)}) copy-start(f32[768,2304]{1,0:T(8,128)S(1)} %convolution_dynamic-update-slice_fusion) | copy-start | bytes 21233668
  72.4 12.7 %collective-permute-start.10 = (f32[768,1024]{1,0:T(8,128)}, f32[768,1024]{1,0:T(8,128)}, u32[]{:S(2)}, u32[]{:S(2)}) collective-permute-start(f32[768,1024]{1,0:T(8,128)} %slice.206), channel_id=1, source_target_pairs={{0,2},{2,0},{4,6},{6,4},{8,10},{10,8},{12,14},{14,12},{16,18},{18,... | collective-permute-start | bytes 9437192 | tf_op jit(solution)/shard_map/ppermute | solution.py:37
  73.8 0.7 copy-start.16
  76.3 4.8 %copy-start.10 = (bf16[256,768]{1,0:T(8,128)(2,1)S(1)}, bf16[256,768]{1,0:T(8,128)(2,1)}, u32[]{:S(2)}) copy-start(bf16[256,768]{1,0:T(8,128)(2,1)} %copy-done.9) | copy-start | bytes 1179652
  76.3 4.8 %copy-start.12 = (bf16[256,768]{1,0:T(8,128)(2,1)S(1)}, bf16[256,768]{1,0:T(8,128)(2,1)}, u32[]{:S(2)}) copy-start(bf16[256,768]{1,0:T(8,128)(2,1)} %copy-done.11) | copy-start | bytes 1179652
  76.3 4.8 %copy-start.19 = (bf16[256,384]{1,0:T(8,128)(2,1)S(1)}, bf16[256,384]{1,0:T(8,128)(2,1)}, u32[]{:S(2)}) copy-start(bf16[256,384]{1,0:T(8,128)(2,1)} %concatenate.46) | copy-start | bytes 589828
  78.6 3.2 %copy-start.4 = (bf16[256,768]{1,0:T(8,128)(2,1)S(1)}, bf16[256,768]{1,0:T(8,128)(2,1)}, u32[]{:S(2)}) copy-start(bf16[256,768]{1,0:T(8,128)(2,1)} %copy-done.3) | copy-start | bytes 1179652
  78.6 3.2 %copy-start.7 = (bf16[256,768]{1,0:T(8,128)(2,1)S(1)}, bf16[256,768]{1,0:T(8,128)(2,1)}, u32[]{:S(2)}) copy-start(bf16[256,768]{1,0:T(8,128)(2,1)} %copy-done.6) | copy-start | bytes 1179652
  78.6 3.2 %copy-start.27 = (pred[256]{0:T(512)(128)(4,1)S(1)}, pred[256]{0:T(512)(128)(4,1)}, u32[]{:S(2)}) copy-start(pred[256]{0:T(512)(128)(4,1)} %copy-done.26) | copy-start | bytes 772
  81.2 0.9 copy-start.17
  84.9 5.0 %collective-permute-start.12 = (f32[4,2,96,768]{3,2,0,1:T(8,128)}, f32[4,2,96,768]{3,2,0,1:T(8,128)}, u32[]{:S(2)}, u32[]{:S(2)}) collective-permute-start(f32[4,2,96,768]{3,2,0,1:T(8,128)} %pad_maximum_fusion), channel_id=1, source_target_pairs={{0,2},{2,0},{4,6},{6,4},{8,10},{10,8},{12,14},{14,12},{16,18},{18,... | collective-permute-start | bytes 7077896 | tf_op jit(solution)/shard_map/ppermute | solution.py:37
  88.2 20.0 %collective-permute-start.11 = (bf16[768,512]{1,0:T(8,128)(2,1)}, bf16[768,512]{1,0:T(8,128)(2,1)}, u32[]{:S(2)}, u32[]{:S(2)}) collective-permute-start(bf16[768,512]{1,0:T(8,128)(2,1)} %fusion.32), channel_id=1, source_target_pairs={{0,4},{2,6},{4,0},{6,2},{8,12},{10,14},{12,8},{14,10},{16,20},{18,... | collective-permute-start | bytes 2359304 | tf_op jit(solution)/shard_map/ppermute | solution.py:37
  109.5 8.2 %copy-start.18 = (bf16[256,384]{0,1:T(8,128)(2,1)S(1)}, bf16[256,384]{0,1:T(8,128)(2,1)}, u32[]{:S(2)}) copy-start(bf16[256,384]{0,1:T(8,128)(2,1)} %fusion.44) | copy-start | bytes 589828
  111.5 13.0 %collective-permute-start.14 = (bf16[768,256]{1,0:T(8,128)(2,1)S(1)}, bf16[768,256]{1,0:T(8,128)(2,1)S(1)}, u32[]{:S(2)}, u32[]{:S(2)}) collective-permute-start(bf16[768,256]{1,0:T(8,128)(2,1)S(1)} %get-tuple-element.21), channel_id=1, source_target_pairs={{8,0},{10,2},{12,4},{14,6},{16,8},{18,10},{20,12},{22,14},{24,16},... | collective-permute-start | bytes 1179656 | tf_op jit(solution)/shard_map/ppermute | solution.py:43
  112.8 12.9 %collective-permute-start.15 = (bf16[768,256]{1,0:T(8,128)(2,1)S(1)}, bf16[768,256]{1,0:T(8,128)(2,1)S(1)}, u32[]{:S(2)}, u32[]{:S(2)}) collective-permute-start(bf16[768,256]{1,0:T(8,128)(2,1)S(1)} %get-tuple-element.22), channel_id=1, source_target_pairs={{0,8},{2,10},{4,12},{6,14},{8,16},{10,18},{12,20},{14,22},{16,24},... | collective-permute-start | bytes 1179656 | tf_op jit(solution)/shard_map/ppermute | solution.py:43
  118.3 9.0 %copy-start.5 = (bf16[256,768]{1,0:T(8,128)(2,1)S(1)}, bf16[256,768]{1,0:T(8,128)(2,1)}, u32[]{:S(2)}) copy-start(bf16[256,768]{1,0:T(8,128)(2,1)} %copy-done.3) | copy-start | bytes 1179652
  118.4 9.0 %copy-start.8 = (bf16[256,768]{1,0:T(8,128)(2,1)S(1)}, bf16[256,768]{1,0:T(8,128)(2,1)}, u32[]{:S(2)}) copy-start(bf16[256,768]{1,0:T(8,128)(2,1)} %copy-done.6) | copy-start | bytes 1179652
  118.4 9.0 %copy-start.28 = (pred[256]{0:T(512)(128)(4,1)S(1)}, pred[256]{0:T(512)(128)(4,1)}, u32[]{:S(2)}) copy-start(pred[256]{0:T(512)(128)(4,1)} %copy-done.26) | copy-start | bytes 772
  118.5 14.4 %collective-permute-start.13 = (bf16[4,96,768]{2,1,0:T(8,128)(2,1)S(1)}, bf16[4,96,768]{2,1,0:T(8,128)(2,1)S(1)}, u32[]{:S(2)}, u32[]{:S(2)}) collective-permute-start(bf16[4,96,768]{2,1,0:T(8,128)(2,1)S(1)} %fusion.52), channel_id=1, source_target_pairs={{0,4},{2,6},{4,0},{6,2},{8,12},{10,14},{12,8},{14,10},{16,20},{18,... | collective-permute-start | bytes 1769480 | tf_op jit(solution)/shard_map/ppermute | solution.py:37
  127.3 1.3 copy-start.13
  129.2 2.6 %copy-start.15 = (bf16[1536,384]{1,0:T(8,128)(2,1)S(1)}, bf16[1536,384]{1,0:T(8,128)(2,1)}, u32[]{:S(2)}) copy-start(bf16[1536,384]{1,0:T(8,128)(2,1)} %param.18) | copy-start | bytes 3538948
where the time goes:
time: 174 us
  waiting for transfers between devices  43.2 us (25%)
  Pallas kernels  38.4 us (22%)
  matrix products  37.6 us (22%)
  starting transfers between devices  22.7 us (13%)
  other arithmetic  18.9 us (11%)
  local copies, waits for them, and re-layouts  10.7 us (6%)
  between operations  2.19 us (1%)
    pallas_call x1, Pallas kernels, closing_sums(): pl.pallas_call(functools.partial(closing_kernel, groups), out_shape=(jax....  38.4 us
    ppermute x12, waiting for transfers between devices, swapped(): lax.ppermute(value, axis, [(source, source ^ bit) for source in range(cou...  30.1 us
    ppermute x4, waiting for transfers between devices, passed_along(): lax.ppermute(value, axis, [(source, source + steps) for source in range(f...  13.1 us
    dot_general x14, matrix products, contract_last(): lax.dot_general(left, right, (((1,), (1,)), ((), ())), preferred_element_...  12.7 us
    ppermute x4, starting transfers between devices, passed_along(): lax.ppermute(value, axis, [(source, source + steps) for source in range(f...  11.6 us
    ppermute x12, starting transfers between devices, swapped(): lax.ppermute(value, axis, [(source, source ^ bit) for source in range(cou...  11.1 us
    dot_general x6, matrix products, body(): jnp.dot(dscore, head_keys, preferred_element_type=jnp.float32)  7.58 us
    dot_general x14, matrix products, contract_first(): lax.dot_general(left, right, (((0,), (0,)), ((), ())), preferred_element_...  6.96 us
  transfers between devices with their start and end apart: 16, of which 9 were waited for; matrix products, arithmetic and copies ran while one was open for 18% of the time, Pallas kernels for 0%

commit v1 on v0

--- a/solution.py
+++ b/solution.py
@@ -105,6 +105,10 @@
     early_recv_sems,
     late_send_sems,
     late_recv_sems,
+    core_send_sems,
+    core_recv_sems,
+    side_send_sems,
+    side_recv_sems,
 ):
     me = lax.axis_index("seq")
     head = lax.axis_index("head")
@@ -135,9 +139,18 @@
         copy.start()
         return copy
 
-    core_copy = remote(
-        late_ref.at[1 - core], core_slot, single_send.at[0], single_recv.at[0], peers[0]
-    )
+    order = targets + [group]
+    core_copies = []
+    for piece, owner in enumerate(order):
+        core_copies.append(
+            remote(
+                late_ref.at[1 - core, owner],
+                core_slot.at[piece],
+                core_send_sems.at[piece],
+                core_recv_sems.at[piece],
+                peers[0],
+            )
+        )
     early_send[...] = early_ref[...].astype(jnp.bfloat16)
     early_copies = []
     for step in range(1, groups):
@@ -150,25 +163,38 @@
                 peers[2 + step],
             )
         )
-    head_copy = remote(sent_ref, head_slot, single_send.at[2], single_recv.at[2], peers[2])
-    core_copy.wait()
-    side_send[...] = (late_ref[core, 1 - side] + core_slot[1 - side]).astype(jnp.bfloat16)
-    side_copy = remote(side_send, side_slot, single_send.at[1], single_recv.at[1], peers[1])
-    total[...] = late_ref[core, side] + core_slot[side]
-    side_copy.wait()
-    total[...] = total[...] + side_slot[...].astype(jnp.float32)
-    late_send[...] = total[...].astype(jnp.bfloat16)
+    head_copy = remote(sent_ref, head_slot, single_send.at[0], single_recv.at[0], peers[2])
+    side_copies = []
+    for piece, owner in enumerate(order):
+        core_copies[piece].wait()
+        side_send[piece] = (
+            late_ref[core, owner, 1 - side] + core_slot[piece, 1 - side]
+        ).astype(jnp.bfloat16)
+        side_copies.append(
+            remote(
+                side_send.at[piece],
+                side_slot.at[piece],
+                side_send_sems.at[piece],
+                side_recv_sems.at[piece],
+                peers[1],
+            )
+        )
+        total[piece] = late_ref[core, owner, side] + core_slot[piece, side]
     late_copies = []
-    for step in range(1, groups):
-        late_copies.append(
-            remote(
-                late_send.at[targets[step - 1]],
-                late_slots.at[step - 1],
-                late_send_sems.at[step - 1],
-                late_recv_sems.at[step - 1],
-                peers[2 + step],
+    for piece in range(groups):
+        side_copies[piece].wait()
+        total[piece] = total[piece] + side_slot[piece].astype(jnp.float32)
+        if piece < groups - 1:
+            late_send[piece] = total[piece].astype(jnp.bfloat16)
+            late_copies.append(
+                remote(
+                    late_send.at[piece],
+                    late_slots.at[piece],
+                    late_send_sems.at[piece],
+                    late_recv_sems.at[piece],
+                    peers[3 + piece],
+                )
             )
-        )
     head_copy.wait()
     summed_out[...] = kept_ref[...] + head_slot[...]
     result = early_ref[group]
@@ -176,7 +202,7 @@
         early_copies[step - 1].wait()
         result = result + early_slots[step - 1].astype(jnp.float32)
     early_out[...] = result
-    result = total[group]
+    result = total[groups - 1]
     for step in range(1, groups):
         late_copies[step - 1].wait()
         result = result + late_slots[step - 1].astype(jnp.float32)
@@ -199,19 +225,23 @@
         scratch_shapes=[
             pltpu.VMEM(chunk, jnp.bfloat16),
             pltpu.VMEM(slots, jnp.bfloat16),
-            pltpu.VMEM((2,) + chunk, jnp.float32),
+            pltpu.VMEM((groups, 2, rows, width), jnp.float32),
             pltpu.VMEM(chunk, jnp.bfloat16),
             pltpu.VMEM(chunk, jnp.bfloat16),
             pltpu.VMEM(chunk, jnp.float32),
             pltpu.VMEM(chunk, jnp.bfloat16),
             pltpu.VMEM(slots, jnp.bfloat16),
             pltpu.VMEM(kept.shape, jnp.float32),
-            pltpu.SemaphoreType.DMA((3,)),
-            pltpu.SemaphoreType.DMA((3,)),
+            pltpu.SemaphoreType.DMA((1,)),
+            pltpu.SemaphoreType.DMA((1,)),
             pltpu.SemaphoreType.DMA((groups - 1,)),
             pltpu.SemaphoreType.DMA((groups - 1,)),
             pltpu.SemaphoreType.DMA((groups - 1,)),
             pltpu.SemaphoreType.DMA((groups - 1,)),
+            pltpu.SemaphoreType.DMA((groups,)),
+            pltpu.SemaphoreType.DMA((groups,)),
+            pltpu.SemaphoreType.DMA((groups,)),
+            pltpu.SemaphoreType.DMA((groups,)),
         ],
         compiler_params=pltpu.CompilerParams(
             collective_id=0, has_side_effects=True, vmem_limit_bytes=48 * 1024 * 1024
@@ -349,7 +379,7 @@
         summed = kept + swapped(sent, "head", 1)
     else:
         rows = late_part.shape[0] // seq_count
-        blocks = late_part.reshape(groups, 2, 2, rows, late_part.shape[1]).transpose(2, 1, 0, 3, 4)
+        blocks = late_part.reshape(groups, 2, 2, rows, late_part.shape[1]).transpose(2, 0, 1, 3, 4)
         early, late, summed = closing_sums(early_part, blocks, kept, sent)
     input_grad = jnp.where(masked[:, None], 0.0, summed).astype(jnp.bfloat16)
     return (

time: 174 us -> 167 us (0.960)
  Pallas kernels: 38.4 us -> 30.7 us
    pallas_call x1, Pallas kernels: 38.4 us -> 30.7 us  [closing_sums(): pl.pallas_call(functools.partial(closing_kernel, groups), out_shape=(jax....]
  transfers between devices with their start and end apart: 16 -> 16, of which waited for: 9 -> 9; matrix products, arithmetic and copies ran while one was open for 18% -> 19% of each run, Pallas kernels for 0% -> 0%
where the time goes in v1:
time: 167 us; the launch traced here: 166 us
  waiting for transfers between devices  43.2 us (26%)
  matrix products  37.6 us (23%)
  Pallas kernels  30.7 us (18%)
  starting transfers between devices  22.7 us (14%)
  other arithmetic  18.9 us (11%)
  local copies, waits for them, and re-layouts  10.7 us (6%)
  between operations  2.19 us (1%)
    pallas_call x1, Pallas kernels, closing_sums(): pl.pallas_call(functools.partial(closing_kernel, groups), out_shape=(jax....  30.7 us
    ppermute x12, waiting for transfers between devices, swapped(): lax.ppermute(value, axis, [(source, source ^ bit) for source in range(cou...  30.1 us
    ppermute x4, waiting for transfers between devices, passed_along(): lax.ppermute(value, axis, [(source, source + steps) for source in range(f...  13.1 us
    dot_general x14, matrix products, contract_last(): lax.dot_general(left, right, (((1,), (1,)), ((), ())), preferred_element_...  12.7 us
    ppermute x4, starting transfers between devices, passed_along(): lax.ppermute(value, axis, [(source, source + steps) for source in range(f...  11.6 us
    ppermute x12, starting transfers between devices, swapped(): lax.ppermute(value, axis, [(source, source ^ bit) for source in range(cou...  11.1 us
    dot_general x6, matrix products, body(): jnp.dot(dscore, head_keys, preferred_element_type=jnp.float32)  7.58 us
    dot_general x14, matrix products, contract_first(): lax.dot_general(left, right, (((0,), (0,)), ((), ())), preferred_element_...  6.96 us
  transfers between devices with their start and end apart: 16, of which 9 were waited for; matrix products, arithmetic and copies ran while one was open for 19% of the time, Pallas kernels for 0%

profile of v1, /device:TPU:0, one launch (start us, length us, event | category | flops | bytes accessed | tf_op | source)
XLA Modules:
  0.0 166.0 jit_solution(15271188732008782739)
XLA Ops:
  0.6 3.0 %collective-permute-start = (bf16[256,768]{1,0:T(8,128)(2,1)}, bf16[256,768]{1,0:T(8,128)(2,1)S(1)}, u32[]{:S(2)}, u32[]{:S(2)}) collective-permute-start(bf16[256,768]{1,0:T(8,128)(2,1)} %param.10), channel_id=1, source_target_pairs={{0,1},{1,0},{2,3},{3,2},{4,5},{5,4},{6,7},{7,6},{8,9},{9,8},{10,11... | collective-permute-start | bytes 1179656 | tf_op jit(solution)/shard_map/ppermute | solution.py:37
  5.1 0.8 convert_reduce_fusion
  5.9 0.7 compare_reduce_fusion
  6.7 7.1 %collective-permute-done = bf16[256,768]{1,0:T(8,128)(2,1)S(1)} collective-permute-done((bf16[256,768]{1,0:T(8,128)(2,1)}, bf16[256,768]{1,0:T(8,128)(2,1)S(1)}, u32[]{:S(2)}, u32[]{:S(2)}) %collective-permute-start) | collective-permute-done | bytes 393248 | tf_op jit(solution)/shard_map/ppermute | solution.py:37
  13.8 1.1 broadcast_select_fusion.5
  14.9 2.2 %convolution_convert_fusion.2 = bf16[256,384]{1,0:T(8,128)(2,1)S(1)} fusion(bf16[1536,384]{1,0:T(8,128)(2,1)} %param.17, bf16[256,768]{1,0:T(8,128)(2,1)S(1)} %get-tuple-element.34, bf16[256,768]{1,0:T(8,128)(2,1)S(1)} %get-tuple-element.33, f32[1536]{0:T(1024)S(1)} %convert_reduce_fusion, f32[1536]{0:T(1024)S(1)} %convert_element_type.146, ...), kind=kOutput, calls=%fused_computation.85 | convolution fusion | flops 304840704 | bytes 2175232 | tf_op jit(solution)/shard_map/dot_general | solution.py:273
  17.8 4.1 %collective-permute-start.1 = (bf16[256,768]{1,0:T(8,128)(2,1)S(1)}, bf16[256,768]{1,0:T(8,128)(2,1)S(1)}, u32[]{:S(2)}, u32[]{:S(2)}) collective-permute-start(bf16[256,768]{1,0:T(8,128)(2,1)S(1)} %pad_maximum_fusion.4), channel_id=1, source_target_pairs={{0,8},{2,10},{4,12},{6,14},{8,16},{10,18},{12,20},{14,22},{16,24},... | collective-permute-start | bytes 1179656 | tf_op jit(solution)/shard_map/ppermute | solution.py:43
  21.9 1.3 collective-permute-start.2
  23.2 1.6 collective-permute-start.5
  24.8 3.4 %collective-permute-done.1 = bf16[256,768]{1,0:T(8,128)(2,1)S(1)} collective-permute-done((bf16[256,768]{1,0:T(8,128)(2,1)S(1)}, bf16[256,768]{1,0:T(8,128)(2,1)S(1)}, u32[]{:S(2)}, u32[]{:S(2)}) %collective-permute-start.1) | collective-permute-done | bytes 393248 | tf_op jit(solution)/shard_map/ppermute | solution.py:43
  28.2 4.1 %collective-permute-done.2 = bf16[256,768]{1,0:T(8,128)(2,1)S(1)} collective-permute-done((bf16[256,768]{1,0:T(8,128)(2,1)S(1)}, bf16[256,768]{1,0:T(8,128)(2,1)S(1)}, u32[]{:S(2)}, u32[]{:S(2)}) %collective-permute-start.2) | collective-permute-done | bytes 393248 | tf_op jit(solution)/shard_map/ppermute | solution.py:43
  32.4 1.6 collective-permute-start.3
  34.7 5.6 %collective-permute-done.3 = bf16[256,768]{1,0:T(8,128)(2,1)S(1)} collective-permute-done((bf16[256,768]{1,0:T(8,128)(2,1)S(1)}, bf16[256,768]{1,0:T(8,128)(2,1)S(1)}, u32[]{:S(2)}, u32[]{:S(2)}) %collective-permute-start.3) | collective-permute-done | bytes 393248 | tf_op jit(solution)/shard_map/ppermute | solution.py:37
  43.1 1.3 fusion.122
  44.4 1.2 fusion.127
  45.6 1.3 fusion.126
  46.9 1.2 fusion.125
  48.0 1.3 fusion.124
  49.3 1.2 fusion.123
  53.7 0.8 convolution_convert_fusion.7
  56.8 1.5 multiply_reduce_fusion
  59.8 0.8 fusion.13
  61.2 0.8 fusion.15
  62.6 0.8 fusion.17
  63.3 0.8 fusion.36
  70.0 2.5 %slice.206 = f32[768,1024]{1,0:T(8,128)} slice(f32[768,2304]{1,0:T(8,128)S(1)} %convolution_dynamic-update-slice_fusion), slice={[0:768], [0:1024]} | slice | bytes 6291456 | tf_op jit(solution)/shard_map/slice | solution.py:346
  72.8 1.0 fusion.40
  74.5 1.8 %concatenate.46 = bf16[256,384]{1,0:T(8,128)(2,1)} concatenate(bf16[256,64]{1,0:T(8,128)(2,1)} %copy-done.24, bf16[256,64]{1,0:T(8,128)(2,1)} %copy-done.23, bf16[256,64]{1,0:T(8,128)(2,1)} %copy-done.22, bf16[256,64]{1,0:T(8,128)(2,1)} %copy-done.21, bf16[256,64]{1,0:T(8,128)(2,1)} %copy-done.20, bf16[256,64]{1,0:T(8,128)(2,1)} %get-tuple-element.53), dimensions={1} | concatenate | bytes 393216 | tf_op jit(solution)/shard_map/concatenate | solution.py:341
  76.3 2.3 %fusion.42 = bf16[256,384]{0,1:T(8,128)(2,1)} fusion(bf16[256,384]{0,1:T(8,128)(2,1)} %copy-done.16, bf16[256,2304]{1,0:T(8,128)(2,1)S(1)} %fusion.16, bf16[2304,768]{1,0:T(8,128)(2,1)} %copy-done.1), kind=kOutput, calls=%fused_computation.108 | convolution fusion | flops 75530240 | bytes 1802240 | tf_op jit(solution)/shard_map/dot_general | solution.py:338
  78.6 2.5 %fusion.44 = bf16[256,384]{0,1:T(8,128)(2,1)} fusion(bf16[256,384]{0,1:T(8,128)(2,1)} %fusion.42, bf16[256,2304]{1,0:T(8,128)(2,1)S(1)} %fusion.17, bf16[2304,768]{1,0:T(8,128)(2,1)} %copy-done.1), kind=kOutput, calls=%fused_computation.110 | convolution fusion | flops 75530240 | bytes 1802240 | tf_op jit(solution)/shard_map/dot_general | solution.py:338
  83.3 1.6 pad_maximum_fusion
  85.2 3.0 %fusion.32 = bf16[768,512]{1,0:T(8,128)(2,1)} fusion(f32[768,2304]{1,0:T(8,128)} %copy-done.2, f32[768,1024]{1,0:T(8,128)} %collective-permute-done.10), kind=kLoop, calls=%fused_computation.75 | loop fusion | flops 786432 | bytes 3932160 | tf_op jit(solution)/shard_map/convert_element_type | solution.py:349
  88.2 1.5 collective-permute-start.11
  89.9 1.9 %maximum_add_fusion = f32[4,2,96,768]{3,2,0,1:T(8,128)S(1)} fusion(f32[4,2,96,768]{3,2,0,1:T(8,128)} %collective-permute-done.12, f32[4,2,96,384]{3,2,0,1:T(8,128)S(1)} %bitcast.53, f32[4,2,96,384]{3,2,0,1:T(8,128)S(1)} %bitcast.54), kind=kLoop, calls=%fused_computation.51 | loop fusion | flops 1179648 | bytes 7077888 | tf_op jit(solution)/shard_map/add | solution.py:63
  91.8 16.4 %collective-permute-done.11 = bf16[768,512]{1,0:T(8,128)(2,1)} collective-permute-done((bf16[768,512]{1,0:T(8,128)(2,1)}, bf16[768,512]{1,0:T(8,128)(2,1)}, u32[]{:S(2)}, u32[]{:S(2)}) %collective-permute-start.11) | collective-permute-done | bytes 786464 | tf_op jit(solution)/shard_map/ppermute | solution.py:37
  108.2 1.3 convert_element_type.187
  109.5 2.0 %fusion.48 = (bf16[768,256]{1,0:T(8,128)(2,1)S(1)}, bf16[768,256]{1,0:T(8,128)(2,1)S(1)}) fusion(f32[768,2304]{1,0:T(8,128)} %copy-done.2, f32[768,512]{1,0:T(8,128)S(1)} %convert_element_type.187, f32[768,1024]{1,0:T(8,128)} %collective-permute-done.10, pred[]{:T(512)S(6)} %eq.44, pred[]{:T(512)S(6)} %eq.45, pred[]{:T(512)S(6)} %eq.47, pred[]{:T(512)S(6)} %eq.46), kind=kLoop, calls=%fused_computation.116 | loop fusion | flops 1966080 | bytes 3932164 | tf_op jit(solution)/shard_map/convert_element_type | solution.py:361
  111.5 1.3 collective-permute-start.14
  112.8 4.9 %collective-permute-start.15 = (bf16[768,256]{1,0:T(8,128)(2,1)S(1)}, bf16[768,256]{1,0:T(8,128)(2,1)S(1)}, u32[]{:S(2)}, u32[]{:S(2)}) collective-permute-start(bf16[768,256]{1,0:T(8,128)(2,1)S(1)} %get-tuple-element.22), channel_id=1, source_target_pairs={{0,8},{2,10},{4,12},{6,14},{8,16},{10,18},{12,20},{14,22},{16,24},... | collective-permute-start | bytes 1179656 | tf_op jit(solution)/shard_map/ppermute | solution.py:43
  118.5 1.6 collective-permute-start.13
  120.0 4.4 %collective-permute-done.14 = bf16[768,256]{1,0:T(8,128)(2,1)S(1)} collective-permute-done((bf16[768,256]{1,0:T(8,128)(2,1)S(1)}, bf16[768,256]{1,0:T(8,128)(2,1)S(1)}, u32[]{:S(2)}, u32[]{:S(2)}) %collective-permute-start.14) | collective-permute-done | bytes 393248 | tf_op jit(solution)/shard_map/ppermute | solution.py:43
  124.4 1.2 collective-permute-done.15
  125.6 1.7 %fusion.51 = bf16[768,256]{1,0:T(8,128)(2,1)S(1)} fusion(f32[768,512]{1,0:T(8,128)S(1)} %convert_element_type.187, f32[768,1024]{1,0:T(8,128)} %collective-permute-done.10, f32[768,2304]{1,0:T(8,128)} %copy-done.2, bf16[768,256]{1,0:T(8,128)(2,1)S(1)} %collective-permute-done.15, bf16[768,256]{1,0:T(8,128)(2,1)S(1)} %collective-permute-done.14), kind=kLoop, calls=%fused_computation.120 | loop fusion | flops 1376256 | bytes 3538944 | tf_op jit(solution)/shard_map/convert_element_type | solution.py:363
  127.3 0.9 fusion.118
  129.2 2.5 %copy.62 = f32[4,2,2,96,768]{4,3,1,0,2:T(8,128)} copy(f32[4,2,2,96,768]{4,3,2,1,0:T(8,128)S(1)} %bitcast.50) | data formatting | bytes 9437184 | tf_op jit(solution)/shard_map/reshape | solution.py:382
  133.0 30.7 %shard_map.137 = (f32[96,768]{1,0:T(8,128)S(1)}, f32[96,768]{1,0:T(8,128)S(1)}, f32[256,768]{1,0:T(8,128)S(1)}) custom-call(f32[4,96,768]{2,1,0:T(8,128)S(1)} %bitcast_add_fusion.early_ref, f32[2,4,2,96,768]{4,3,2,1,0:T(8,128)} %bitcast.49, f32[256,768]{1,0:T(8,128)S(1)} %get-tuple-element.28.kept_ref, f32[256,768]{1,0:T(8,128)S(1)} %get-tuple-element.27.sent_ref), custom_call_target="tpu_custom_call" | custom-call | tf_op jit(solution)/shard_map/pallas_call | solution.py:216
  163.7 0.9 select_convert_fusion
  165.3 0.7 fusion.121
  (151 shorter events, 26.0 us)
Async XLA Ops:
  0.6 39.7 %copy-start = (bf16[1536,384]{1,0:T(8,128)(2,1)S(1)}, bf16[1536,384]{1,0:T(8,128)(2,1)}, u32[]{:S(2)}) copy-start(bf16[1536,384]{1,0:T(8,128)(2,1)} %param.16) | copy-start | bytes 3538948
  0.6 13.2 %collective-permute-start = (bf16[256,768]{1,0:T(8,128)(2,1)}, bf16[256,768]{1,0:T(8,128)(2,1)S(1)}, u32[]{:S(2)}, u32[]{:S(2)}) collective-permute-start(bf16[256,768]{1,0:T(8,128)(2,1)} %param.10), channel_id=1, source_target_pairs={{0,1},{1,0},{2,3},{3,2},{4,5},{5,4},{6,7},{7,6},{8,9},{9,8},{10,11... | collective-permute-start | bytes 1179656 | tf_op jit(solution)/shard_map/ppermute | solution.py:37
  3.6 30.4 %collective-permute-start.9 = (bf16[256,768]{1,0:T(8,128)(2,1)}, bf16[256,768]{1,0:T(8,128)(2,1)S(1)}, u32[]{:S(2)}, u32[]{:S(2)}) collective-permute-start(bf16[256,768]{1,0:T(8,128)(2,1)} %param.11), channel_id=1, source_target_pairs={{0,1},{1,0},{2,3},{3,2},{4,5},{5,4},{6,7},{7,6},{8,9},{9,8},{10,11... | collective-permute-start | bytes 1179656 | tf_op jit(solution)/shard_map/ppermute | solution.py:37
  6.7 33.6 %copy-start.26 = (pred[256]{0:T(512)(128)(4,1)}, pred[256]{0:T(512)(128)(4,1)S(1)}, u32[]{:S(2)}) copy-start(pred[256]{0:T(512)(128)(4,1)S(1)} %compare_reduce_fusion) | copy-start | bytes 772
  14.9 25.4 %copy-start.3 = (bf16[256,768]{1,0:T(8,128)(2,1)}, bf16[256,768]{1,0:T(8,128)(2,1)S(1)}, u32[]{:S(2)}) copy-start(bf16[256,768]{1,0:T(8,128)(2,1)S(1)} %get-tuple-element.33) | copy-start | bytes 1179652
  14.9 25.4 %copy-start.6 = (bf16[256,768]{1,0:T(8,128)(2,1)}, bf16[256,768]{1,0:T(8,128)(2,1)S(1)}, u32[]{:S(2)}) copy-start(bf16[256,768]{1,0:T(8,128)(2,1)S(1)} %get-tuple-element.34) | copy-start | bytes 1179652
  14.9 2.2 %copy-start.14 = (bf16[1536,384]{1,0:T(8,128)(2,1)S(1)}, bf16[1536,384]{1,0:T(8,128)(2,1)}, u32[]{:S(2)}) copy-start(bf16[1536,384]{1,0:T(8,128)(2,1)} %param.18) | copy-start | bytes 3538948
  17.1 16.9 %copy-start.25 = (bf16[256,768]{1,0:T(8,128)(2,1)S(1)}, bf16[256,768]{1,0:T(8,128)(2,1)}, u32[]{:S(2)}) copy-start(bf16[256,768]{1,0:T(8,128)(2,1)} %param.11) | copy-start | bytes 1179652
  17.8 10.4 %collective-permute-start.1 = (bf16[256,768]{1,0:T(8,128)(2,1)S(1)}, bf16[256,768]{1,0:T(8,128)(2,1)S(1)}, u32[]{:S(2)}, u32[]{:S(2)}) collective-permute-start(bf16[256,768]{1,0:T(8,128)(2,1)S(1)} %pad_maximum_fusion.4), channel_id=1, source_target_pairs={{0,8},{2,10},{4,12},{6,14},{8,16},{10,18},{12,20},{14,22},{16,24},... | collective-permute-start | bytes 1179656 | tf_op jit(solution)/shard_map/ppermute | solution.py:43
  21.9 10.5 %collective-permute-start.2 = (bf16[256,768]{1,0:T(8,128)(2,1)S(1)}, bf16[256,768]{1,0:T(8,128)(2,1)S(1)}, u32[]{:S(2)}, u32[]{:S(2)}) collective-permute-start(bf16[256,768]{1,0:T(8,128)(2,1)S(1)} %pad_maximum_fusion.4), channel_id=1, source_target_pairs={{8,0},{10,2},{12,4},{14,6},{16,8},{18,10},{20,12},{22,14},{24,16},... | collective-permute-start | bytes 1179656 | tf_op jit(solution)/shard_map/ppermute | solution.py:43
  23.2 10.9 %collective-permute-start.5 = (bf16[256,768]{1,0:T(8,128)(2,1)S(1)}, bf16[256,768]{1,0:T(8,128)(2,1)S(1)}, u32[]{:S(2)}, u32[]{:S(2)}) collective-permute-start(bf16[256,768]{1,0:T(8,128)(2,1)S(1)} %pad_maximum_fusion.4), channel_id=1, source_target_pairs={{0,4},{2,6},{4,0},{6,2},{8,12},{10,14},{12,8},{14,10},{16,20},{18,... | collective-permute-start | bytes 1179656 | tf_op jit(solution)/shard_map/ppermute | solution.py:37
  32.4 7.9 %collective-permute-start.3 = (bf16[256,768]{1,0:T(8,128)(2,1)S(1)}, bf16[256,768]{1,0:T(8,128)(2,1)S(1)}, u32[]{:S(2)}, u32[]{:S(2)}) collective-permute-start(bf16[256,768]{1,0:T(8,128)(2,1)S(1)} %get-tuple-element.32), channel_id=1, source_target_pairs={{0,4},{2,6},{4,0},{6,2},{8,12},{10,14},{12,8},{14,10},{16,20},{18,... | collective-permute-start | bytes 1179656 | tf_op jit(solution)/shard_map/ppermute | solution.py:37
  34.0 8.9 %collective-permute-start.8 = (bf16[256,768]{1,0:T(8,128)(2,1)S(1)}, bf16[256,768]{1,0:T(8,128)(2,1)S(1)}, u32[]{:S(2)}, u32[]{:S(2)}) collective-permute-start(bf16[256,768]{1,0:T(8,128)(2,1)S(1)} %pad_maximum_fusion.4), channel_id=1, source_target_pairs={{0,2},{2,0},{4,6},{6,4},{8,10},{10,8},{12,14},{14,12},{16,18},{18,... | collective-permute-start | bytes 1179656 | tf_op jit(solution)/shard_map/ppermute | solution.py:37
  34.1 8.0 %copy-start.9 = (bf16[256,768]{1,0:T(8,128)(2,1)}, bf16[256,768]{1,0:T(8,128)(2,1)S(1)}, u32[]{:S(2)}) copy-start(bf16[256,768]{1,0:T(8,128)(2,1)S(1)} %get-tuple-element.29) | copy-start | bytes 1179652
  34.1 8.0 %copy-start.11 = (bf16[256,768]{1,0:T(8,128)(2,1)}, bf16[256,768]{1,0:T(8,128)(2,1)S(1)}, u32[]{:S(2)}) copy-start(bf16[256,768]{1,0:T(8,128)(2,1)S(1)} %get-tuple-element.30) | copy-start | bytes 1179652
  34.1 7.4 %copy-start.29 = (bf16[384,1536]{1,0:T(8,128)(2,1)S(1)}, bf16[384,1536]{1,0:T(8,128)(2,1)}, u32[]{:S(2)}) copy-start(bf16[384,1536]{1,0:T(8,128)(2,1)} %param.19) | copy-start | bytes 3538948
  34.1 8.0 %collective-permute-start.6 = (bf16[256,768]{1,0:T(8,128)(2,1)S(1)}, bf16[256,768]{1,0:T(8,128)(2,1)S(1)}, u32[]{:S(2)}, u32[]{:S(2)}) collective-permute-start(bf16[256,768]{1,0:T(8,128)(2,1)S(1)} %collective-permute-done.5), channel_id=1, source_target_pairs={{0,2},{2,0},{4,6},{6,4},{8,10},{10,8},{12,14},{14,12},{16,18},{18,... | collective-permute-start | bytes 1179656 | tf_op jit(solution)/shard_map/ppermute | solution.py:37
  40.3 1.8 %collective-permute-start.4 = (bf16[256,768]{1,0:T(8,128)(2,1)S(1)}, bf16[256,768]{1,0:T(8,128)(2,1)S(1)}, u32[]{:S(2)}, u32[]{:S(2)}) collective-permute-start(bf16[256,768]{1,0:T(8,128)(2,1)S(1)} %collective-permute-done.3), channel_id=1, source_target_pairs={{0,2},{2,0},{4,6},{6,4},{8,10},{10,8},{12,14},{14,12},{16,18},{18,... | collective-permute-start | bytes 1179656 | tf_op jit(solution)/shard_map/ppermute | solution.py:37
  41.0 1.9 %collective-permute-start.7 = (bf16[256,768]{1,0:T(8,128)(2,1)S(1)}, bf16[256,768]{1,0:T(8,128)(2,1)S(1)}, u32[]{:S(2)}, u32[]{:S(2)}) collective-permute-start(bf16[256,768]{1,0:T(8,128)(2,1)S(1)} %get-tuple-element.31), channel_id=1, source_target_pairs={{0,2},{2,0},{4,6},{6,4},{8,10},{10,8},{12,14},{14,12},{16,18},{18,... | collective-permute-start | bytes 1179656 | tf_op jit(solution)/shard_map/ppermute | solution.py:37
  43.1 29.7 %copy-start.1 = (bf16[2304,768]{1,0:T(8,128)(2,1)}, bf16[2304,768]{1,0:T(8,128)(2,1)S(1)}, u32[]{:S(2)}) copy-start(bf16[2304,768]{1,0:T(8,128)(2,1)S(1)} %constant_dynamic-update-slice_fusion.1) | copy-start | bytes 10616836
  52.1 4.7 %copy-start.20 = (bf16[256,64]{1,0:T(8,128)(2,1)}, bf16[256,64]{1,0:T(8,128)(2,1)S(1)}, u32[]{:S(2)}) copy-start(bf16[256,64]{1,0:T(8,128)(2,1)S(1)} %convolution_convert_fusion.5) | copy-start | bytes 98308
  53.2 3.5 %copy-start.21 = (bf16[256,64]{1,0:T(8,128)(2,1)}, bf16[256,64]{1,0:T(8,128)(2,1)S(1)}, u32[]{:S(2)}) copy-start(bf16[256,64]{1,0:T(8,128)(2,1)S(1)} %convolution_convert_fusion.6) | copy-start | bytes 98308
  54.5 2.3 %copy-start.22 = (bf16[256,64]{1,0:T(8,128)(2,1)}, bf16[256,64]{1,0:T(8,128)(2,1)S(1)}, u32[]{:S(2)}) copy-start(bf16[256,64]{1,0:T(8,128)(2,1)S(1)} %convolution_convert_fusion.7) | copy-start | bytes 98308
  55.7 1.1 copy-start.23
  56.8 2.1 %copy-start.24 = (bf16[256,64]{1,0:T(8,128)(2,1)}, bf16[256,64]{1,0:T(8,128)(2,1)S(1)}, u32[]{:S(2)}) copy-start(bf16[256,64]{1,0:T(8,128)(2,1)S(1)} %convolution_convert_fusion.9) | copy-start | bytes 98308
  70.0 3.9 %copy-start.2 = (f32[768,2304]{1,0:T(8,128)}, f32[768,2304]{1,0:T(8,128)S(1)}, u32[]{:S(2)}) copy-start(f32[768,2304]{1,0:T(8,128)S(1)} %convolution_dynamic-update-slice_fusion) | copy-start | bytes 21233668
  72.4 12.7 %collective-permute-start.10 = (f32[768,1024]{1,0:T(8,128)}, f32[768,1024]{1,0:T(8,128)}, u32[]{:S(2)}, u32[]{:S(2)}) collective-permute-start(f32[768,1024]{1,0:T(8,128)} %slice.206), channel_id=1, source_target_pairs={{0,2},{2,0},{4,6},{6,4},{8,10},{10,8},{12,14},{14,12},{16,18},{18,... | collective-permute-start | bytes 9437192 | tf_op jit(solution)/shard_map/ppermute | solution.py:37
  73.8 0.7 copy-start.16
  76.3 4.8 %copy-start.10 = (bf16[256,768]{1,0:T(8,128)(2,1)S(1)}, bf16[256,768]{1,0:T(8,128)(2,1)}, u32[]{:S(2)}) copy-start(bf16[256,768]{1,0:T(8,128)(2,1)} %copy-done.9) | copy-start | bytes 1179652
  76.3 4.8 %copy-start.12 = (bf16[256,768]{1,0:T(8,128)(2,1)S(1)}, bf16[256,768]{1,0:T(8,128)(2,1)}, u32[]{:S(2)}) copy-start(bf16[256,768]{1,0:T(8,128)(2,1)} %copy-done.11) | copy-start | bytes 1179652
  76.3 4.8 %copy-start.19 = (bf16[256,384]{1,0:T(8,128)(2,1)S(1)}, bf16[256,384]{1,0:T(8,128)(2,1)}, u32[]{:S(2)}) copy-start(bf16[256,384]{1,0:T(8,128)(2,1)} %concatenate.46) | copy-start | bytes 589828
  78.6 3.2 %copy-start.4 = (bf16[256,768]{1,0:T(8,128)(2,1)S(1)}, bf16[256,768]{1,0:T(8,128)(2,1)}, u32[]{:S(2)}) copy-start(bf16[256,768]{1,0:T(8,128)(2,1)} %copy-done.3) | copy-start | bytes 1179652
  78.6 3.2 %copy-start.7 = (bf16[256,768]{1,0:T(8,128)(2,1)S(1)}, bf16[256,768]{1,0:T(8,128)(2,1)}, u32[]{:S(2)}) copy-start(bf16[256,768]{1,0:T(8,128)(2,1)} %copy-done.6) | copy-start | bytes 1179652
  78.6 3.2 %copy-start.27 = (pred[256]{0:T(512)(128)(4,1)S(1)}, pred[256]{0:T(512)(128)(4,1)}, u32[]{:S(2)}) copy-start(pred[256]{0:T(512)(128)(4,1)} %copy-done.26) | copy-start | bytes 772
  81.2 0.9 copy-start.17
  84.9 5.0 %collective-permute-start.12 = (f32[4,2,96,768]{3,2,0,1:T(8,128)}, f32[4,2,96,768]{3,2,0,1:T(8,128)}, u32[]{:S(2)}, u32[]{:S(2)}) collective-permute-start(f32[4,2,96,768]{3,2,0,1:T(8,128)} %pad_maximum_fusion), channel_id=1, source_target_pairs={{0,2},{2,0},{4,6},{6,4},{8,10},{10,8},{12,14},{14,12},{16,18},{18,... | collective-permute-start | bytes 7077896 | tf_op jit(solution)/shard_map/ppermute | solution.py:37
  88.2 20.0 %collective-permute-start.11 = (bf16[768,512]{1,0:T(8,128)(2,1)}, bf16[768,512]{1,0:T(8,128)(2,1)}, u32[]{:S(2)}, u32[]{:S(2)}) collective-permute-start(bf16[768,512]{1,0:T(8,128)(2,1)} %fusion.32), channel_id=1, source_target_pairs={{0,4},{2,6},{4,0},{6,2},{8,12},{10,14},{12,8},{14,10},{16,20},{18,... | collective-permute-start | bytes 2359304 | tf_op jit(solution)/shard_map/ppermute | solution.py:37
  109.5 8.2 %copy-start.18 = (bf16[256,384]{0,1:T(8,128)(2,1)S(1)}, bf16[256,384]{0,1:T(8,128)(2,1)}, u32[]{:S(2)}) copy-start(bf16[256,384]{0,1:T(8,128)(2,1)} %fusion.44) | copy-start | bytes 589828
  111.5 13.0 %collective-permute-start.14 = (bf16[768,256]{1,0:T(8,128)(2,1)S(1)}, bf16[768,256]{1,0:T(8,128)(2,1)S(1)}, u32[]{:S(2)}, u32[]{:S(2)}) collective-permute-start(bf16[768,256]{1,0:T(8,128)(2,1)S(1)} %get-tuple-element.21), channel_id=1, source_target_pairs={{8,0},{10,2},{12,4},{14,6},{16,8},{18,10},{20,12},{22,14},{24,16},... | collective-permute-start | bytes 1179656 | tf_op jit(solution)/shard_map/ppermute | solution.py:43
  112.8 12.9 %collective-permute-start.15 = (bf16[768,256]{1,0:T(8,128)(2,1)S(1)}, bf16[768,256]{1,0:T(8,128)(2,1)S(1)}, u32[]{:S(2)}, u32[]{:S(2)}) collective-permute-start(bf16[768,256]{1,0:T(8,128)(2,1)S(1)} %get-tuple-element.22), channel_id=1, source_target_pairs={{0,8},{2,10},{4,12},{6,14},{8,16},{10,18},{12,20},{14,22},{16,24},... | collective-permute-start | bytes 1179656 | tf_op jit(solution)/shard_map/ppermute | solution.py:43
  118.3 9.0 %copy-start.5 = (bf16[256,768]{1,0:T(8,128)(2,1)S(1)}, bf16[256,768]{1,0:T(8,128)(2,1)}, u32[]{:S(2)}) copy-start(bf16[256,768]{1,0:T(8,128)(2,1)} %copy-done.3) | copy-start | bytes 1179652
  118.4 9.0 %copy-start.8 = (bf16[256,768]{1,0:T(8,128)(2,1)S(1)}, bf16[256,768]{1,0:T(8,128)(2,1)}, u32[]{:S(2)}) copy-start(bf16[256,768]{1,0:T(8,128)(2,1)} %copy-done.6) | copy-start | bytes 1179652
  118.4 9.0 %copy-start.28 = (pred[256]{0:T(512)(128)(4,1)S(1)}, pred[256]{0:T(512)(128)(4,1)}, u32[]{:S(2)}) copy-start(pred[256]{0:T(512)(128)(4,1)} %copy-done.26) | copy-start | bytes 772
  118.5 14.4 %collective-permute-start.13 = (bf16[4,96,768]{2,1,0:T(8,128)(2,1)S(1)}, bf16[4,96,768]{2,1,0:T(8,128)(2,1)S(1)}, u32[]{:S(2)}, u32[]{:S(2)}) collective-permute-start(bf16[4,96,768]{2,1,0:T(8,128)(2,1)S(1)} %fusion.52), channel_id=1, source_target_pairs={{0,4},{2,6},{4,0},{6,2},{8,12},{10,14},{12,8},{14,10},{16,20},{18,... | collective-permute-start | bytes 1769480 | tf_op jit(solution)/shard_map/ppermute | solution.py:37
  127.3 1.3 copy-start.13
  129.2 2.6 %copy-start.15 = (bf16[1536,384]{1,0:T(8,128)(2,1)S(1)}, bf16[1536,384]{1,0:T(8,128)(2,1)}, u32[]{:S(2)}) copy-start(bf16[1536,384]{1,0:T(8,128)(2,1)} %param.18) | copy-start | bytes 3538948

commit v2 on v1

--- a/solution.py
+++ b/solution.py
@@ -350,11 +350,12 @@
     early_part = core_summed(
         [contract_first(hidden, query_rounded), contract_first(full_grad, attn_out)], seq_index
     )
-    by_side, early_part = lax.optimization_barrier((swapped(for_side, "seq", 2), early_part))
-    by_side = by_side.astype(jnp.float32)
+    side_far = swapped(for_side[:, :slab_rows], "seq", 2)
+    side_own = swapped(for_side[:, slab_rows:], "seq", 2).astype(jnp.float32)
+    side_far, early_part = lax.optimization_barrier((side_far, early_part))
+    side_far = side_far.astype(jnp.float32)
     early_part = side_summed(early_part, seq_index)
     core_far, core_own = by_core[:, 2 * slab_rows : 3 * slab_rows], by_core[:, 3 * slab_rows :]
-    side_far, side_own = by_side[:, :slab_rows], by_side[:, slab_rows:]
     to_below = slab_of(7, 1) + jnp.where(core == 1, core_far, 0.0) + jnp.where(side == 1, side_far, 0.0)
     to_above = slab_of(8, 1) + jnp.where(core == 0, core_far, 0.0) + jnp.where(side == 0, side_far, 0.0)
     slab_total = slab_of(6, 1) + core_own + side_own

time: 167 us -> 176 us (1.054)
  matrix products: 37.6 us -> 55.9 us
  waiting for transfers between devices: 43.2 us -> 34.8 us
  other arithmetic: 18.9 us -> 17.1 us
    dot_general x14, matrix products: 6.96 us -> 18.5 us  [contract_first(): lax.dot_general(left, right, (((0,), (0,)), ((), ())), preferred_element_...]
    ppermute x12 -> x13, waiting for transfers between devices: 30.1 us -> 22.1 us  [swapped(): lax.ppermute(value, axis, [(source, source ^ bit) for source in range(cou...]
    dot_general x14, matrix products: 12.7 us -> 17.9 us  [contract_last(): lax.dot_general(left, right, (((1,), (1,)), ((), ())), preferred_element_...]
    ppermute x12 -> x13, starting transfers between devices: 11.1 us -> 11.7 us  [swapped(): lax.ppermute(value, axis, [(source, source ^ bit) for source in range(cou...]
  transfers between devices with their start and end apart: 16 -> 17, of which waited for: 9 -> 10; matrix products, arithmetic and copies ran while one was open for 19% -> 15% of each run, Pallas kernels for 0% -> 0%
where the time goes in v2:
time: 176 us; the launch traced here: 175 us
  matrix products  55.9 us (32%)
  waiting for transfers between devices  34.8 us (20%)
  Pallas kernels  30.4 us (17%)
  starting transfers between devices  23.2 us (13%)
  other arithmetic  17.1 us (10%)
  local copies, waits for them, and re-layouts  11.2 us (6%)
  between operations  2.4 us (1%)
    pallas_call x1, Pallas kernels, closing_sums(): pl.pallas_call(functools.partial(closing_kernel, groups), out_shape=(jax....  30.4 us
    ppermute x13, waiting for transfers between devices, swapped(): lax.ppermute(value, axis, [(source, source ^ bit) for source in range(cou...  22.1 us
    dot_general x14, matrix products, contract_first(): lax.dot_general(left, right, (((0,), (0,)), ((), ())), preferred_element_...  18.5 us
    dot_general x14, matrix products, contract_last(): lax.dot_general(left, right, (((1,), (1,)), ((), ())), preferred_element_...  17.9 us
    ppermute x4, waiting for transfers between devices, passed_along(): lax.ppermute(value, axis, [(source, source + steps) for source in range(f...  12.7 us
    ppermute x13, starting transfers between devices, swapped(): lax.ppermute(value, axis, [(source, source ^ bit) for source in range(cou...  11.7 us
    ppermute x4, starting transfers between devices, passed_along(): lax.ppermute(value, axis, [(source, source + steps) for source in range(f...  11.6 us
    dot_general x6, matrix products, body(): jnp.dot(dscore, head_keys, preferred_element_type=jnp.float32)  9.15 us
  transfers between devices with their start and end apart: 17, of which 10 were waited for; matrix products, arithmetic and copies ran while one was open for 15% of the time, Pallas kernels for 0%

profile of v2, /device:TPU:0, one launch (start us, length us, event | category | flops | bytes accessed | tf_op | source)
XLA Modules:
  0.0 174.9 jit_solution(1844519382836175461)
XLA Ops:
  0.6 3.0 %collective-permute-start = (bf16[256,768]{1,0:T(8,128)(2,1)}, bf16[256,768]{1,0:T(8,128)(2,1)S(1)}, u32[]{:S(2)}, u32[]{:S(2)}) collective-permute-start(bf16[256,768]{1,0:T(8,128)(2,1)} %param.10), channel_id=1, source_target_pairs={{0,1},{1,0},{2,3},{3,2},{4,5},{5,4},{6,7},{7,6},{8,9},{9,8},{10,11... | collective-permute-start | bytes 1179656 | tf_op jit(solution)/shard_map/ppermute | solution.py:37
  6.7 7.1 %collective-permute-done = bf16[256,768]{1,0:T(8,128)(2,1)S(1)} collective-permute-done((bf16[256,768]{1,0:T(8,128)(2,1)}, bf16[256,768]{1,0:T(8,128)(2,1)S(1)}, u32[]{:S(2)}, u32[]{:S(2)}) %collective-permute-start) | collective-permute-done | bytes 393248 | tf_op jit(solution)/shard_map/ppermute | solution.py:37
  14.9 2.2 %convolution_convert_fusion.2 = bf16[256,384]{1,0:T(8,128)(2,1)S(1)} fusion(bf16[1536,384]{1,0:T(8,128)(2,1)} %param.17, bf16[256,768]{1,0:T(8,128)(2,1)S(1)} %get-tuple-element.36, bf16[256,768]{1,0:T(8,128)(2,1)S(1)} %get-tuple-element.35, f32[1536]{0:T(1024)S(1)} %convert_reduce_fusion, f32[1536]{0:T(1024)S(1)} %convert_element_type.149, ...), kind=kOutput, calls=%fused_computation.85 | convolution fusion | flops 304840704 | bytes 2175232 | tf_op jit(solution)/shard_map/dot_general | solution.py:273
  17.8 4.1 %collective-permute-start.1 = (bf16[256,768]{1,0:T(8,128)(2,1)S(1)}, bf16[256,768]{1,0:T(8,128)(2,1)S(1)}, u32[]{:S(2)}, u32[]{:S(2)}) collective-permute-start(bf16[256,768]{1,0:T(8,128)(2,1)S(1)} %pad_maximum_fusion.4), channel_id=1, source_target_pairs={{0,8},{2,10},{4,12},{6,14},{8,16},{10,18},{12,20},{14,22},{16,24},... | collective-permute-start | bytes 1179656 | tf_op jit(solution)/shard_map/ppermute | solution.py:43
  21.9 1.3 collective-permute-start.2
  23.2 1.6 collective-permute-start.5
  24.8 3.4 %collective-permute-done.1 = bf16[256,768]{1,0:T(8,128)(2,1)S(1)} collective-permute-done((bf16[256,768]{1,0:T(8,128)(2,1)S(1)}, bf16[256,768]{1,0:T(8,128)(2,1)S(1)}, u32[]{:S(2)}, u32[]{:S(2)}) %collective-permute-start.1) | collective-permute-done | bytes 393248 | tf_op jit(solution)/shard_map/ppermute | solution.py:43
  28.2 4.1 %collective-permute-done.2 = bf16[256,768]{1,0:T(8,128)(2,1)S(1)} collective-permute-done((bf16[256,768]{1,0:T(8,128)(2,1)S(1)}, bf16[256,768]{1,0:T(8,128)(2,1)S(1)}, u32[]{:S(2)}, u32[]{:S(2)}) %collective-permute-start.2) | collective-permute-done | bytes 393248 | tf_op jit(solution)/shard_map/ppermute | solution.py:43
  32.4 1.6 collective-permute-start.3
  34.7 5.6 %collective-permute-done.3 = bf16[256,768]{1,0:T(8,128)(2,1)S(1)} collective-permute-done((bf16[256,768]{1,0:T(8,128)(2,1)S(1)}, bf16[256,768]{1,0:T(8,128)(2,1)S(1)}, u32[]{:S(2)}, u32[]{:S(2)}) %collective-permute-start.3) | collective-permute-done | bytes 393248 | tf_op jit(solution)/shard_map/ppermute | solution.py:37
  43.6 1.3 fusion.124
  46.1 1.3 fusion.128
  48.6 1.3 fusion.126
  57.3 1.4 multiply_reduce_fusion
  60.5 1.2 fusion.23
  61.7 1.8 %fusion.13 = bf16[256,2304]{1,0:T(8,128)(2,1)} fusion(f32[256,2304]{1,0:T(8,128)S(1)} %get-tuple-element.48, f32[256]{0:T(256)S(1)} %get-tuple-element.17, f32[256]{0:T(256)S(1)} %log_add_fusion.4, bf16[2304,768]{1,0:T(8,128)(2,1)S(1)} %constant_dynamic-update-slice_fusion.1, bf16[256,384]{1,0:T(8,128)(2,1)S(1)} %convolution_convert_fusion), kind=kOutput, calls=%fused_computation.26 | convolution fusion | flops 77856768 | bytes 4196352 | tf_op jit(solution)/shard_map/dot_general | solution.py:24
  63.5 1.7 fusion.14
  65.2 1.9 %fusion.15 = bf16[256,2304]{1,0:T(8,128)(2,1)} fusion(f32[256,2304]{1,0:T(8,128)S(1)} %get-tuple-element.52, f32[256]{0:T(256)S(1)} %get-tuple-element.19, f32[256]{0:T(256)S(1)} %log_add_fusion.2, bf16[2304,768]{1,0:T(8,128)(2,1)S(1)} %constant_dynamic-update-slice_fusion.1, bf16[256,384]{1,0:T(8,128)(2,1)S(1)} %convolution_convert_fusion), kind=kOutput, calls=%fused_computation.28 | convolution fusion | flops 77856768 | bytes 4196352 | tf_op jit(solution)/shard_map/dot_general | solution.py:24
  67.1 1.7 fusion.16
  68.8 1.8 %fusion.17 = bf16[256,2304]{1,0:T(8,128)(2,1)} fusion(f32[256,2304]{1,0:T(8,128)S(1)} %get-tuple-element.44, f32[256]{0:T(256)S(1)} %get-tuple-element.15, f32[256]{0:T(256)S(1)} %log_add_fusion, bf16[2304,768]{1,0:T(8,128)(2,1)S(1)} %constant_dynamic-update-slice_fusion.1, bf16[256,384]{1,0:T(8,128)(2,1)S(1)} %convolution_convert_fusion), kind=kOutput, calls=%fused_computation.30 | convolution fusion | flops 77856768 | bytes 4196352 | tf_op jit(solution)/shard_map/dot_general | solution.py:24
  70.5 1.8 %concatenate.46 = bf16[256,384]{1,0:T(8,128)(2,1)} concatenate(bf16[256,64]{1,0:T(8,128)(2,1)} %copy-done.44, bf16[256,64]{1,0:T(8,128)(2,1)} %copy-done.43, bf16[256,64]{1,0:T(8,128)(2,1)} %copy-done.42, bf16[256,64]{1,0:T(8,128)(2,1)} %copy-done.41, bf16[256,64]{1,0:T(8,128)(2,1)} %copy-done.40, bf16[256,64]{1,0:T(8,128)(2,1)} %get-tuple-element.55), dimensions={1} | concatenate | bytes 393216 | tf_op jit(solution)/shard_map/concatenate | solution.py:341
  72.3 3.0 %fusion.36 = bf16[256,384]{0,1:T(8,128)(2,1)} fusion(bf16[256,384]{0,1:T(8,128)(2,1)} %fusion.34, bf16[256,2304]{1,0:T(8,128)(2,1)} %fusion.13, bf16[2304,768]{1,0:T(8,128)(2,1)} %copy-done.11), kind=kOutput, calls=%fused_computation.102 | convolution fusion | flops 75530240 | bytes 1802240 | tf_op jit(solution)/shard_map/dot_general | solution.py:338
  75.3 2.7 %fusion.22 = f32[768,2304]{1,0:T(8,128)} fusion(f32[768,2304]{1,0:T(8,128)} %fusion.23, bf16[256,2304]{1,0:T(8,128)(2,1)} %fusion.13, bf16[256,384]{1,0:T(8,128)(2,1)} %copy-done.37), kind=kOutput, calls=%fused_computation.46 | convolution fusion | flops 75644928 | bytes 1835008 | tf_op jit(solution)/shard_map/dot_general | solution.py:18
  78.0 2.4 %fusion.38 = bf16[256,384]{0,1:T(8,128)(2,1)} fusion(bf16[256,384]{0,1:T(8,128)(2,1)} %fusion.36, bf16[256,2304]{1,0:T(8,128)(2,1)} %fusion.14, bf16[2304,768]{1,0:T(8,128)(2,1)S(1)} %copy-done.12), kind=kOutput, calls=%fused_computation.104 | convolution fusion | flops 75530240 | bytes 1802240 | tf_op jit(solution)/shard_map/dot_general | solution.py:338
  80.4 1.2 fusion.21
  81.6 1.4 fusion.40
  83.0 1.3 fusion.20
  85.4 1.2 fusion.18
  86.7 1.4 convolution_dynamic-update-slice_fusion.5
  88.1 1.4 convolution_dynamic-update-slice_fusion.4
  89.5 1.4 convolution_dynamic-update-slice_fusion.3
  90.9 1.4 convolution_dynamic-update-slice_fusion.2
  92.3 1.6 convolution_dynamic-update-slice_fusion.1
  93.9 1.4 convolution_dynamic-update-slice_fusion
  95.2 2.3 %slice.206 = f32[768,1024]{1,0:T(8,128)S(1)} slice(f32[768,2304]{1,0:T(8,128)} %convolution_dynamic-update-slice_fusion), slice={[0:768], [0:1024]} | slice | bytes 6291456 | tf_op jit(solution)/shard_map/slice | solution.py:346
  101.3 1.7 pad_maximum_fusion
  103.3 2.8 %fusion.32 = bf16[768,512]{1,0:T(8,128)(2,1)S(1)} fusion(f32[768,2304]{1,0:T(8,128)} %convolution_dynamic-update-slice_fusion, f32[768,1024]{1,0:T(8,128)S(1)} %collective-permute-done.10), kind=kLoop, calls=%fused_computation.75 | loop fusion | flops 786432 | bytes 3932160 | tf_op jit(solution)/shard_map/convert_element_type | solution.py:349
  107.1 1.5 collective-permute-start.11
  108.8 2.1 %maximum_add_fusion = f32[4,2,96,768]{3,2,0,1:T(8,128)S(1)} fusion(f32[4,2,96,768]{3,2,0,1:T(8,128)} %collective-permute-done.12, f32[4,2,96,384]{3,2,0,1:T(8,128)S(1)} %bitcast.53, f32[4,2,96,384]{3,2,0,1:T(8,128)S(1)} %bitcast.54), kind=kLoop, calls=%fused_computation.51 | loop fusion | flops 1179648 | bytes 7077888 | tf_op jit(solution)/shard_map/add | solution.py:63
  111.5 7.8 %collective-permute-done.11 = bf16[768,256]{1,0:T(8,128)(2,1)} collective-permute-done((bf16[768,256]{1,0:T(8,128)(2,1)}, bf16[768,256]{1,0:T(8,128)(2,1)}, u32[]{:S(2)}, u32[]{:S(2)}) %collective-permute-start.11) | collective-permute-done | bytes 393248 | tf_op jit(solution)/shard_map/ppermute | solution.py:37
  119.4 1.8 %fusion.46 = (bf16[768,256]{1,0:T(8,128)(2,1)S(1)}, bf16[768,256]{1,0:T(8,128)(2,1)S(1)}) fusion(bf16[768,256]{1,0:T(8,128)(2,1)} %collective-permute-done.11, f32[768,2304]{1,0:T(8,128)} %convolution_dynamic-update-slice_fusion, f32[768,1024]{1,0:T(8,128)S(1)} %copy-done.26, pred[]{:T(512)S(6)} %eq.44, pred[]{:T(512)S(6)} %eq.45, pred[]{:T(512)S(6)} %eq.47, ...), kind=kLoop, calls=%fused_computation.114 | loop fusion | flops 2162688 | bytes 3538948 | tf_op jit(solution)/shard_map/convert_element_type | solution.py:362
  121.1 1.3 collective-permute-start.15
  122.4 4.9 %collective-permute-start.16 = (bf16[768,256]{1,0:T(8,128)(2,1)S(1)}, bf16[768,256]{1,0:T(8,128)(2,1)S(1)}, u32[]{:S(2)}, u32[]{:S(2)}) collective-permute-start(bf16[768,256]{1,0:T(8,128)(2,1)S(1)} %get-tuple-element.22), channel_id=1, source_target_pairs={{0,8},{2,10},{4,12},{6,14},{8,16},{10,18},{12,20},{14,22},{16,24},... | collective-permute-start | bytes 1179656 | tf_op jit(solution)/shard_map/ppermute | solution.py:43
  128.1 1.6 collective-permute-start.13
  129.7 4.0 %collective-permute-done.15 = bf16[768,256]{1,0:T(8,128)(2,1)S(1)} collective-permute-done((bf16[768,256]{1,0:T(8,128)(2,1)S(1)}, bf16[768,256]{1,0:T(8,128)(2,1)S(1)}, u32[]{:S(2)}, u32[]{:S(2)}) %collective-permute-start.15) | collective-permute-done | bytes 393248 | tf_op jit(solution)/shard_map/ppermute | solution.py:43
  134.8 1.4 fusion.52
  138.1 2.6 %copy.62 = f32[4,2,2,96,768]{4,3,1,0,2:T(8,128)} copy(f32[4,2,2,96,768]{4,3,2,1,0:T(8,128)S(1)} %bitcast.50) | data formatting | bytes 9437184 | tf_op jit(solution)/shard_map/reshape | solution.py:383
  142.2 30.4 %shard_map.137 = (f32[96,768]{1,0:T(8,128)S(1)}, f32[96,768]{1,0:T(8,128)S(1)}, f32[256,768]{1,0:T(8,128)S(1)}) custom-call(f32[4,96,768]{2,1,0:T(8,128)S(1)} %bitcast_add_fusion.early_ref, f32[2,4,2,96,768]{4,3,2,1,0:T(8,128)} %bitcast.49, f32[256,768]{1,0:T(8,128)S(1)} %get-tuple-element.28.kept_ref, f32[256,768]{1,0:T(8,128)S(1)} %get-tuple-element.27.sent_ref), custom_call_target="tpu_custom_call" | custom-call | tf_op jit(solution)/shard_map/pallas_call | solution.py:216
  (227 shorter events, 33.8 us)
Async XLA Ops:
  0.6 39.7 %copy-start = (bf16[1536,384]{1,0:T(8,128)(2,1)S(1)}, bf16[1536,384]{1,0:T(8,128)(2,1)}, u32[]{:S(2)}) copy-start(bf16[1536,384]{1,0:T(8,128)(2,1)} %param.16) | copy-start | bytes 3538948
  0.6 13.2 %collective-permute-start = (bf16[256,768]{1,0:T(8,128)(2,1)}, bf16[256,768]{1,0:T(8,128)(2,1)S(1)}, u32[]{:S(2)}, u32[]{:S(2)}) collective-permute-start(bf16[256,768]{1,0:T(8,128)(2,1)} %param.10), channel_id=1, source_target_pairs={{0,1},{1,0},{2,3},{3,2},{4,5},{5,4},{6,7},{7,6},{8,9},{9,8},{10,11... | collective-permute-start | bytes 1179656 | tf_op jit(solution)/shard_map/ppermute | solution.py:37
  3.6 30.4 %collective-permute-start.9 = (bf16[256,768]{1,0:T(8,128)(2,1)}, bf16[256,768]{1,0:T(8,128)(2,1)S(1)}, u32[]{:S(2)}, u32[]{:S(2)}) collective-permute-start(bf16[256,768]{1,0:T(8,128)(2,1)} %param.11), channel_id=1, source_target_pairs={{0,1},{1,0},{2,3},{3,2},{4,5},{5,4},{6,7},{7,6},{8,9},{9,8},{10,11... | collective-permute-start | bytes 1179656 | tf_op jit(solution)/shard_map/ppermute | solution.py:37
  3.7 13.4 %copy-start.64 = (s32[256]{0:T(256)}, s32[256]{0:T(256)S(1)}, u32[]{:S(2)}) copy-start(s32[256]{0:T(256)S(1)} %iota_add_fusion) | copy-start | bytes 3076
  6.7 33.6 %copy-start.61 = (pred[256]{0:T(512)(128)(4,1)}, pred[256]{0:T(512)(128)(4,1)S(1)}, u32[]{:S(2)}) copy-start(pred[256]{0:T(512)(128)(4,1)S(1)} %compare_reduce_fusion) | copy-start | bytes 772
  14.9 25.5 %copy-start.19 = (bf16[256,768]{1,0:T(8,128)(2,1)}, bf16[256,768]{1,0:T(8,128)(2,1)S(1)}, u32[]{:S(2)}) copy-start(bf16[256,768]{1,0:T(8,128)(2,1)S(1)} %get-tuple-element.35) | copy-start | bytes 1179652
  14.9 25.4 %copy-start.22 = (bf16[256,768]{1,0:T(8,128)(2,1)}, bf16[256,768]{1,0:T(8,128)(2,1)S(1)}, u32[]{:S(2)}) copy-start(bf16[256,768]{1,0:T(8,128)(2,1)S(1)} %get-tuple-element.36) | copy-start | bytes 1179652
  17.1 16.9 %copy-start.45 = (bf16[256,768]{1,0:T(8,128)(2,1)S(1)}, bf16[256,768]{1,0:T(8,128)(2,1)}, u32[]{:S(2)}) copy-start(bf16[256,768]{1,0:T(8,128)(2,1)} %param.11) | copy-start | bytes 1179652
  17.8 10.4 %collective-permute-start.1 = (bf16[256,768]{1,0:T(8,128)(2,1)S(1)}, bf16[256,768]{1,0:T(8,128)(2,1)S(1)}, u32[]{:S(2)}, u32[]{:S(2)}) collective-permute-start(bf16[256,768]{1,0:T(8,128)(2,1)S(1)} %pad_maximum_fusion.4), channel_id=1, source_target_pairs={{0,8},{2,10},{4,12},{6,14},{8,16},{10,18},{12,20},{14,22},{16,24},... | collective-permute-start | bytes 1179656 | tf_op jit(solution)/shard_map/ppermute | solution.py:43
  21.9 10.5 %collective-permute-start.2 = (bf16[256,768]{1,0:T(8,128)(2,1)S(1)}, bf16[256,768]{1,0:T(8,128)(2,1)S(1)}, u32[]{:S(2)}, u32[]{:S(2)}) collective-permute-start(bf16[256,768]{1,0:T(8,128)(2,1)S(1)} %pad_maximum_fusion.4), channel_id=1, source_target_pairs={{8,0},{10,2},{12,4},{14,6},{16,8},{18,10},{20,12},{22,14},{24,16},... | collective-permute-start | bytes 1179656 | tf_op jit(solution)/shard_map/ppermute | solution.py:43
  23.2 17.7 %copy-start.59 = (s32[2304]{0:T(1024)}, s32[2304]{0:T(1024)S(1)}, u32[]{:S(2)}) copy-start(s32[2304]{0:T(1024)S(1)} %constant_dynamic-update-slice_fusion.12) | copy-start | bytes 27652
  23.2 10.9 %collective-permute-start.5 = (bf16[256,768]{1,0:T(8,128)(2,1)S(1)}, bf16[256,768]{1,0:T(8,128)(2,1)S(1)}, u32[]{:S(2)}, u32[]{:S(2)}) collective-permute-start(bf16[256,768]{1,0:T(8,128)(2,1)S(1)} %pad_maximum_fusion.4), channel_id=1, source_target_pairs={{0,4},{2,6},{4,0},{6,2},{8,12},{10,14},{12,8},{14,10},{16,20},{18,... | collective-permute-start | bytes 1179656 | tf_op jit(solution)/shard_map/ppermute | solution.py:37
  32.4 7.9 %collective-permute-start.3 = (bf16[256,768]{1,0:T(8,128)(2,1)S(1)}, bf16[256,768]{1,0:T(8,128)(2,1)S(1)}, u32[]{:S(2)}, u32[]{:S(2)}) collective-permute-start(bf16[256,768]{1,0:T(8,128)(2,1)S(1)} %get-tuple-element.34), channel_id=1, source_target_pairs={{0,4},{2,6},{4,0},{6,2},{8,12},{10,14},{12,8},{14,10},{16,20},{18,... | collective-permute-start | bytes 1179656 | tf_op jit(solution)/shard_map/ppermute | solution.py:37
  34.0 9.0 %collective-permute-start.8 = (bf16[256,768]{1,0:T(8,128)(2,1)S(1)}, bf16[256,768]{1,0:T(8,128)(2,1)S(1)}, u32[]{:S(2)}, u32[]{:S(2)}) collective-permute-start(bf16[256,768]{1,0:T(8,128)(2,1)S(1)} %pad_maximum_fusion.4), channel_id=1, source_target_pairs={{0,2},{2,0},{4,6},{6,4},{8,10},{10,8},{12,14},{14,12},{16,18},{18,... | collective-permute-start | bytes 1179656 | tf_op jit(solution)/shard_map/ppermute | solution.py:37
  34.1 8.0 %copy-start.27 = (bf16[256,768]{1,0:T(8,128)(2,1)}, bf16[256,768]{1,0:T(8,128)(2,1)S(1)}, u32[]{:S(2)}) copy-start(bf16[256,768]{1,0:T(8,128)(2,1)S(1)} %get-tuple-element.31) | copy-start | bytes 1179652
  34.1 8.0 %copy-start.29 = (bf16[256,768]{1,0:T(8,128)(2,1)}, bf16[256,768]{1,0:T(8,128)(2,1)S(1)}, u32[]{:S(2)}) copy-start(bf16[256,768]{1,0:T(8,128)(2,1)S(1)} %get-tuple-element.32) | copy-start | bytes 1179652
  34.1 7.4 %copy-start.66 = (bf16[384,1536]{1,0:T(8,128)(2,1)S(1)}, bf16[384,1536]{1,0:T(8,128)(2,1)}, u32[]{:S(2)}) copy-start(bf16[384,1536]{1,0:T(8,128)(2,1)} %param.19) | copy-start | bytes 3538948
  34.1 8.1 %collective-permute-start.6 = (bf16[256,768]{1,0:T(8,128)(2,1)S(1)}, bf16[256,768]{1,0:T(8,128)(2,1)S(1)}, u32[]{:S(2)}, u32[]{:S(2)}) collective-permute-start(bf16[256,768]{1,0:T(8,128)(2,1)S(1)} %collective-permute-done.5), channel_id=1, source_target_pairs={{0,2},{2,0},{4,6},{6,4},{8,10},{10,8},{12,14},{14,12},{16,18},{18,... | collective-permute-start | bytes 1179656 | tf_op jit(solution)/shard_map/ppermute | solution.py:37
  40.3 1.9 %collective-permute-start.4 = (bf16[256,768]{1,0:T(8,128)(2,1)S(1)}, bf16[256,768]{1,0:T(8,128)(2,1)S(1)}, u32[]{:S(2)}, u32[]{:S(2)}) collective-permute-start(bf16[256,768]{1,0:T(8,128)(2,1)S(1)} %collective-permute-done.3), channel_id=1, source_target_pairs={{0,2},{2,0},{4,6},{6,4},{8,10},{10,8},{12,14},{14,12},{16,18},{18,... | collective-permute-start | bytes 1179656 | tf_op jit(solution)/shard_map/ppermute | solution.py:37
  41.0 19.5 %copy-start.37 = (bf16[256,384]{1,0:T(8,128)(2,1)}, bf16[256,384]{1,0:T(8,128)(2,1)S(1)}, u32[]{:S(2)}) copy-start(bf16[256,384]{1,0:T(8,128)(2,1)S(1)} %convolution_convert_fusion.3) | copy-start | bytes 589828
  41.0 1.9 %collective-permute-start.7 = (bf16[256,768]{1,0:T(8,128)(2,1)S(1)}, bf16[256,768]{1,0:T(8,128)(2,1)S(1)}, u32[]{:S(2)}, u32[]{:S(2)}) collective-permute-start(bf16[256,768]{1,0:T(8,128)(2,1)S(1)} %get-tuple-element.33), channel_id=1, source_target_pairs={{0,2},{2,0},{4,6},{6,4},{8,10},{10,8},{12,14},{14,12},{16,18},{18,... | collective-permute-start | bytes 1179656 | tf_op jit(solution)/shard_map/ppermute | solution.py:37
  42.2 26.6 %copy-start.17 = (bf16[256,384]{1,0:T(8,128)(2,1)}, bf16[256,384]{1,0:T(8,128)(2,1)S(1)}, u32[]{:S(2)}) copy-start(bf16[256,384]{1,0:T(8,128)(2,1)S(1)} %convolution_convert_fusion) | copy-start | bytes 589828
  43.2 25.6 %copy-start.11 = (bf16[2304,768]{1,0:T(8,128)(2,1)}, bf16[2304,768]{1,0:T(8,128)(2,1)S(1)}, u32[]{:S(2)}) copy-start(bf16[2304,768]{1,0:T(8,128)(2,1)S(1)} %constant_dynamic-update-slice_fusion.1) | copy-start | bytes 10616836
  46.1 21.0 %copy-start.1 = (f32[256,2304]{1,0:T(8,128)}, f32[256,2304]{1,0:T(8,128)S(1)}, u32[]{:S(2)}) copy-start(f32[256,2304]{1,0:T(8,128)S(1)} %get-tuple-element.54) | copy-start | bytes 7077892
  47.4 17.8 %copy-start.3 = (f32[256,2304]{1,0:T(8,128)}, f32[256,2304]{1,0:T(8,128)S(1)}, u32[]{:S(2)}) copy-start(f32[256,2304]{1,0:T(8,128)S(1)} %get-tuple-element.52) | copy-start | bytes 7077892
  48.5 15.0 %copy-start.5 = (f32[256,2304]{1,0:T(8,128)}, f32[256,2304]{1,0:T(8,128)S(1)}, u32[]{:S(2)}) copy-start(f32[256,2304]{1,0:T(8,128)S(1)} %get-tuple-element.50) | copy-start | bytes 7077892
  49.8 11.9 %copy-start.7 = (f32[256,2304]{1,0:T(8,128)}, f32[256,2304]{1,0:T(8,128)S(1)}, u32[]{:S(2)}) copy-start(f32[256,2304]{1,0:T(8,128)S(1)} %get-tuple-element.48) | copy-start | bytes 7077892
  51.0 7.8 %copy-start.9 = (f32[256,2304]{1,0:T(8,128)}, f32[256,2304]{1,0:T(8,128)S(1)}, u32[]{:S(2)}) copy-start(f32[256,2304]{1,0:T(8,128)S(1)} %get-tuple-element.46) | copy-start | bytes 7077892
  51.5 17.3 %copy-start.47 = (f32[256]{0:T(256)}, f32[256]{0:T(256)S(1)}, u32[]{:S(2)}) copy-start(f32[256]{0:T(256)S(1)} %log_add_fusion) | copy-start | bytes 3076
  52.0 15.1 %copy-start.49 = (f32[256]{0:T(256)}, f32[256]{0:T(256)S(1)}, u32[]{:S(2)}) copy-start(f32[256]{0:T(256)S(1)} %log_add_fusion.1) | copy-start | bytes 3076
  53.1 12.1 %copy-start.51 = (f32[256]{0:T(256)}, f32[256]{0:T(256)S(1)}, u32[]{:S(2)}) copy-start(f32[256]{0:T(256)S(1)} %log_add_fusion.2) | copy-start | bytes 3076
  54.2 9.3 %copy-start.53 = (f32[256]{0:T(256)}, f32[256]{0:T(256)S(1)}, u32[]{:S(2)}) copy-start(f32[256]{0:T(256)S(1)} %log_add_fusion.3) | copy-start | bytes 3076
  55.5 6.2 %copy-start.55 = (f32[256]{0:T(256)}, f32[256]{0:T(256)S(1)}, u32[]{:S(2)}) copy-start(f32[256]{0:T(256)S(1)} %log_add_fusion.4) | copy-start | bytes 3076
  72.3 8.0 %copy-start.16 = (bf16[256,2304]{1,0:T(8,128)(2,1)S(1)}, bf16[256,2304]{1,0:T(8,128)(2,1)}, u32[]{:S(2)}) copy-start(bf16[256,2304]{1,0:T(8,128)(2,1)} %fusion.14) | copy-start | bytes 3538948
  72.3 8.0 %copy-start.38 = (bf16[256,384]{1,0:T(8,128)(2,1)S(1)}, bf16[256,384]{1,0:T(8,128)(2,1)}, u32[]{:S(2)}) copy-start(bf16[256,384]{1,0:T(8,128)(2,1)} %copy-done.37) | copy-start | bytes 589828
  75.3 6.3 %copy-start.15 = (bf16[256,2304]{1,0:T(8,128)(2,1)S(1)}, bf16[256,2304]{1,0:T(8,128)(2,1)}, u32[]{:S(2)}) copy-start(bf16[256,2304]{1,0:T(8,128)(2,1)} %fusion.15) | copy-start | bytes 3538948
  97.6 5.7 %collective-permute-start.10 = (f32[768,1024]{1,0:T(8,128)S(1)}, f32[768,1024]{1,0:T(8,128)S(1)}, u32[]{:S(2)}, u32[]{:S(2)}) collective-permute-start(f32[768,1024]{1,0:T(8,128)S(1)} %slice.206), channel_id=1, source_target_pairs={{0,2},{2,0},{4,6},{6,4},{8,10},{10,8},{12,14},{14,12},{16,18},{18,... | collective-permute-start | bytes 9437192 | tf_op jit(solution)/shard_map/ppermute | solution.py:37
  102.9 5.9 %collective-permute-start.12 = (f32[4,2,96,768]{3,2,0,1:T(8,128)}, f32[4,2,96,768]{3,2,0,1:T(8,128)}, u32[]{:S(2)}, u32[]{:S(2)}) collective-permute-start(f32[4,2,96,768]{3,2,0,1:T(8,128)} %pad_maximum_fusion), channel_id=1, source_target_pairs={{0,2},{2,0},{4,6},{6,4},{8,10},{10,8},{12,14},{14,12},{16,18},{18,... | collective-permute-start | bytes 7077896 | tf_op jit(solution)/shard_map/ppermute | solution.py:37
  107.1 12.3 %collective-permute-start.11 = (bf16[768,256]{1,0:T(8,128)(2,1)}, bf16[768,256]{1,0:T(8,128)(2,1)}, u32[]{:S(2)}, u32[]{:S(2)}) collective-permute-start(bf16[768,256]{1,0:T(8,128)(2,1)} %get-tuple-element.30), channel_id=1, source_target_pairs={{0,4},{2,6},{4,0},{6,2},{8,12},{10,14},{12,8},{14,10},{16,20},{18,... | collective-permute-start | bytes 1179656 | tf_op jit(solution)/shard_map/ppermute | solution.py:37
  108.8 10.5 %copy-start.26 = (f32[768,1024]{1,0:T(8,128)S(1)}, f32[768,1024]{1,0:T(8,128)}, u32[]{:S(2)}) copy-start(f32[768,1024]{1,0:T(8,128)} %copy-done.25) | copy-start | bytes 9437188
  110.9 16.4 %copy-start.36 = (bf16[256,384]{0,1:T(8,128)(2,1)S(1)}, bf16[256,384]{0,1:T(8,128)(2,1)}, u32[]{:S(2)}) copy-start(bf16[256,384]{0,1:T(8,128)(2,1)} %copy-done.35) | copy-start | bytes 589828
  110.9 18.7 %collective-permute-start.14 = (bf16[768,256]{1,0:T(8,128)(2,1)S(1)}, bf16[768,256]{1,0:T(8,128)(2,1)S(1)}, u32[]{:S(2)}, u32[]{:S(2)}) collective-permute-start(bf16[768,256]{1,0:T(8,128)(2,1)S(1)} %copy-done.46), channel_id=1, source_target_pairs={{0,4},{2,6},{4,0},{6,2},{8,12},{10,14},{12,8},{14,10},{16,20},{18,... | collective-permute-start | bytes 1179656 | tf_op jit(solution)/shard_map/ppermute | solution.py:37
  121.1 12.5 %collective-permute-start.15 = (bf16[768,256]{1,0:T(8,128)(2,1)S(1)}, bf16[768,256]{1,0:T(8,128)(2,1)S(1)}, u32[]{:S(2)}, u32[]{:S(2)}) collective-permute-start(bf16[768,256]{1,0:T(8,128)(2,1)S(1)} %get-tuple-element.21), channel_id=1, source_target_pairs={{8,0},{10,2},{12,4},{14,6},{16,8},{18,10},{20,12},{22,14},{24,16},... | collective-permute-start | bytes 1179656 | tf_op jit(solution)/shard_map/ppermute | solution.py:43
  122.4 12.4 %collective-permute-start.16 = (bf16[768,256]{1,0:T(8,128)(2,1)S(1)}, bf16[768,256]{1,0:T(8,128)(2,1)S(1)}, u32[]{:S(2)}, u32[]{:S(2)}) collective-permute-start(bf16[768,256]{1,0:T(8,128)(2,1)S(1)} %get-tuple-element.22), channel_id=1, source_target_pairs={{0,8},{2,10},{4,12},{6,14},{8,16},{10,18},{12,20},{14,22},{16,24},... | collective-permute-start | bytes 1179656 | tf_op jit(solution)/shard_map/ppermute | solution.py:43
  128.0 8.2 %copy-start.21 = (bf16[256,768]{1,0:T(8,128)(2,1)S(1)}, bf16[256,768]{1,0:T(8,128)(2,1)}, u32[]{:S(2)}) copy-start(bf16[256,768]{1,0:T(8,128)(2,1)} %copy-done.19) | copy-start | bytes 1179652
  128.0 8.2 %copy-start.24 = (bf16[256,768]{1,0:T(8,128)(2,1)S(1)}, bf16[256,768]{1,0:T(8,128)(2,1)}, u32[]{:S(2)}) copy-start(bf16[256,768]{1,0:T(8,128)(2,1)} %copy-done.22) | copy-start | bytes 1179652
  128.0 8.2 %copy-start.63 = (pred[256]{0:T(512)(128)(4,1)S(1)}, pred[256]{0:T(512)(128)(4,1)}, u32[]{:S(2)}) copy-start(pred[256]{0:T(512)(128)(4,1)} %copy-done.61) | copy-start | bytes 772
  128.1 14.0 %collective-permute-start.13 = (bf16[4,96,768]{2,1,0:T(8,128)(2,1)S(1)}, bf16[4,96,768]{2,1,0:T(8,128)(2,1)S(1)}, u32[]{:S(2)}, u32[]{:S(2)}) collective-permute-start(bf16[4,96,768]{2,1,0:T(8,128)(2,1)S(1)} %fusion.53), channel_id=1, source_target_pairs={{0,4},{2,6},{4,0},{6,2},{8,12},{10,14},{12,8},{14,10},{16,20},{18,... | collective-permute-start | bytes 1769480 | tf_op jit(solution)/shard_map/ppermute | solution.py:37
  (36 other events, 92.1 us)

commit v3 on v1

--- a/solution.py
+++ b/solution.py
@@ -347,6 +347,9 @@
 
     by_core = swapped(slab_of(0, 4), "seq", 1)
     for_side = (by_core[:, : 2 * slab_rows] + slab_of(4, 2)).astype(jnp.bfloat16)
+    for_side, query_rounded, attn_out = lax.optimization_barrier(
+        (for_side, query_rounded, attn_out)
+    )
     early_part = core_summed(
         [contract_first(hidden, query_rounded), contract_first(full_grad, attn_out)], seq_index
     )

time: 167 us -> 179 us (1.072)
  waiting for transfers between devices: 43.2 us -> 53.1 us
  local copies, waits for them, and re-layouts: 10.7 us -> 14.4 us
    ppermute x12, waiting for transfers between devices: 30.1 us -> 39 us  [swapped(): lax.ppermute(value, axis, [(source, source ^ bit) for source in range(cou...]
    unnamed x71 -> x81, local copies, waits for them, and re-layouts: 1.95 us -> 6.13 us
  transfers between devices with their start and end apart: 16 -> 16, of which waited for: 9 -> 11; matrix products, arithmetic and copies ran while one was open for 19% -> 13% of each run, Pallas kernels for 0% -> 0%
where the time goes in v3:
time: 179 us; the launch traced here: 178 us
  waiting for transfers between devices  53.1 us (30%)
  matrix products  36.7 us (21%)
  Pallas kernels  30.5 us (17%)
  starting transfers between devices  21.9 us (12%)
  other arithmetic  19.2 us (11%)
  local copies, waits for them, and re-layouts  14.4 us (8%)
  between operations  2.23 us (1%)
    ppermute x12, waiting for transfers between devices, swapped(): lax.ppermute(value, axis, [(source, source ^ bit) for source in range(cou...  39 us
    pallas_call x1, Pallas kernels, closing_sums(): pl.pallas_call(functools.partial(closing_kernel, groups), out_shape=(jax....  30.5 us
    ppermute x4, waiting for transfers between devices, passed_along(): lax.ppermute(value, axis, [(source, source + steps) for source in range(f...  14.1 us
    dot_general x14, matrix products, contract_last(): lax.dot_general(left, right, (((1,), (1,)), ((), ())), preferred_element_...  12.6 us
    ppermute x12, starting transfers between devices, swapped(): lax.ppermute(value, axis, [(source, source ^ bit) for source in range(cou...  11 us
    ppermute x4, starting transfers between devices, passed_along(): lax.ppermute(value, axis, [(source, source + steps) for source in range(f...  10.9 us
    dot_general x6, matrix products, body(): jnp.dot(dscore, head_keys, preferred_element_type=jnp.float32)  8.32 us
    dot_general x14, matrix products, contract_first(): lax.dot_general(left, right, (((0,), (0,)), ((), ())), preferred_element_...  6.95 us
  transfers between devices with their start and end apart: 16, of which 11 were waited for; matrix products, arithmetic and copies ran while one was open for 13% of the time, Pallas kernels for 0%

profile of v3, /device:TPU:0, one launch (start us, length us, event | category | flops | bytes accessed | tf_op | source)
XLA Modules:
  0.0 178.0 jit_solution(14862824961724880247)
XLA Ops:
  0.7 3.0 %collective-permute-start = (bf16[256,768]{1,0:T(8,128)(2,1)}, bf16[256,768]{1,0:T(8,128)(2,1)S(1)}, u32[]{:S(2)}, u32[]{:S(2)}) collective-permute-start(bf16[256,768]{1,0:T(8,128)(2,1)} %param.10), channel_id=1, source_target_pairs={{0,1},{1,0},{2,3},{3,2},{4,5},{5,4},{6,7},{7,6},{8,9},{9,8},{10,11... | collective-permute-start | bytes 1179656 | tf_op jit(solution)/shard_map/ppermute | solution.py:37
  5.1 0.8 convert_reduce_fusion
  6.7 7.2 %collective-permute-done = bf16[256,768]{1,0:T(8,128)(2,1)S(1)} collective-permute-done((bf16[256,768]{1,0:T(8,128)(2,1)}, bf16[256,768]{1,0:T(8,128)(2,1)S(1)}, u32[]{:S(2)}, u32[]{:S(2)}) %collective-permute-start) | collective-permute-done | bytes 393248 | tf_op jit(solution)/shard_map/ppermute | solution.py:37
  13.8 7.6 %collective-permute-done.9 = bf16[256,768]{1,0:T(8,128)(2,1)S(1)} collective-permute-done((bf16[256,768]{1,0:T(8,128)(2,1)}, bf16[256,768]{1,0:T(8,128)(2,1)S(1)}, u32[]{:S(2)}, u32[]{:S(2)}) %collective-permute-start.9) | collective-permute-done | bytes 393248 | tf_op jit(solution)/shard_map/ppermute | solution.py:37
  21.4 1.2 broadcast_select_fusion.3
  23.3 1.1 copy-done.21
  25.2 3.8 %collective-permute-start.1 = (bf16[256,768]{1,0:T(8,128)(2,1)S(1)}, bf16[256,768]{1,0:T(8,128)(2,1)S(1)}, u32[]{:S(2)}, u32[]{:S(2)}) collective-permute-start(bf16[256,768]{1,0:T(8,128)(2,1)S(1)} %pad_maximum_fusion.4), channel_id=1, source_target_pairs={{0,8},{2,10},{4,12},{6,14},{8,16},{10,18},{12,20},{14,22},{16,24},... | collective-permute-start | bytes 1179656 | tf_op jit(solution)/shard_map/ppermute | solution.py:43
  28.9 1.3 collective-permute-start.2
  30.3 1.6 collective-permute-start.5
  31.9 4.5 %collective-permute-done.1 = bf16[256,768]{1,0:T(8,128)(2,1)S(1)} collective-permute-done((bf16[256,768]{1,0:T(8,128)(2,1)S(1)}, bf16[256,768]{1,0:T(8,128)(2,1)S(1)}, u32[]{:S(2)}, u32[]{:S(2)}) %collective-permute-start.1) | collective-permute-done | bytes 393248 | tf_op jit(solution)/shard_map/ppermute | solution.py:43
  36.4 4.1 %collective-permute-done.2 = bf16[256,768]{1,0:T(8,128)(2,1)S(1)} collective-permute-done((bf16[256,768]{1,0:T(8,128)(2,1)S(1)}, bf16[256,768]{1,0:T(8,128)(2,1)S(1)}, u32[]{:S(2)}, u32[]{:S(2)}) %collective-permute-start.2) | collective-permute-done | bytes 393248 | tf_op jit(solution)/shard_map/ppermute | solution.py:43
  40.6 1.6 collective-permute-start.3
  42.8 6.7 %collective-permute-done.3 = bf16[256,768]{1,0:T(8,128)(2,1)S(1)} collective-permute-done((bf16[256,768]{1,0:T(8,128)(2,1)S(1)}, bf16[256,768]{1,0:T(8,128)(2,1)S(1)}, u32[]{:S(2)}, u32[]{:S(2)}) %collective-permute-start.3) | collective-permute-done | bytes 393248 | tf_op jit(solution)/shard_map/ppermute | solution.py:37
  52.3 1.3 fusion.122
  53.6 1.2 fusion.127
  54.8 1.3 fusion.126
  56.0 1.2 fusion.125
  57.2 1.3 fusion.124
  58.5 1.2 fusion.123
  62.9 0.8 convolution_convert_fusion.7
  66.0 1.5 multiply_reduce_fusion
  77.3 2.9 %copy-done.8 = f32[768,2304]{1,0:T(8,128)} copy-done((f32[768,2304]{1,0:T(8,128)}, f32[768,2304]{1,0:T(8,128)S(1)}, u32[]{:S(2)}) %copy-start.8) | copy-done | bytes 7077912
  80.2 2.0 %slice.206 = f32[768,1024]{1,0:T(8,128)} slice(f32[768,2304]{1,0:T(8,128)S(1)} %convolution_dynamic-update-slice_fusion), slice={[0:768], [0:1024]} | slice | bytes 6291456 | tf_op jit(solution)/shard_map/slice | solution.py:346
  82.6 1.8 %concatenate.46 = bf16[256,384]{1,0:T(8,128)(2,1)} concatenate(bf16[256,64]{1,0:T(8,128)(2,1)} %copy-done.30, bf16[256,64]{1,0:T(8,128)(2,1)} %copy-done.29, bf16[256,64]{1,0:T(8,128)(2,1)} %copy-done.28, bf16[256,64]{1,0:T(8,128)(2,1)} %copy-done.27, bf16[256,64]{1,0:T(8,128)(2,1)} %copy-done.26, bf16[256,64]{1,0:T(8,128)(2,1)} %get-tuple-element.59), dimensions={1} | concatenate | bytes 393216 | tf_op jit(solution)/shard_map/concatenate | solution.py:341
  84.4 2.1 %fusion.34 = bf16[256,384]{0,1:T(8,128)(2,1)S(1)} fusion(bf16[256,2304]{1,0:T(8,128)(2,1)} %copy-done.6, bf16[2304,768]{1,0:T(8,128)(2,1)} %copy-done.1), kind=kOutput, calls=%fused_computation.100 | convolution fusion | flops 75530240 | bytes 1802240 | tf_op jit(solution)/shard_map/dot_general | solution.py:338
  86.5 2.2 %fusion.36 = bf16[256,384]{0,1:T(8,128)(2,1)S(1)} fusion(bf16[256,384]{0,1:T(8,128)(2,1)S(1)} %fusion.34, bf16[256,2304]{1,0:T(8,128)(2,1)} %copy-done.7, bf16[2304,768]{1,0:T(8,128)(2,1)} %copy-done.1), kind=kOutput, calls=%fused_computation.102 | convolution fusion | flops 75530240 | bytes 1802240 | tf_op jit(solution)/shard_map/dot_general | solution.py:338
  88.7 1.8 fusion.38
  90.5 1.0 fusion.40
  92.0 0.8 fusion.44
  92.9 3.1 %fusion.32 = bf16[768,512]{1,0:T(8,128)(2,1)} fusion(f32[768,2304]{1,0:T(8,128)} %copy-done.8, f32[768,1024]{1,0:T(8,128)} %collective-permute-done.10), kind=kLoop, calls=%fused_computation.75 | loop fusion | flops 786432 | bytes 3932160 | tf_op jit(solution)/shard_map/convert_element_type | solution.py:349
  97.0 0.9 copy-done.16
  98.9 1.7 pad_maximum_fusion
  100.7 1.5 collective-permute-start.11
  102.4 3.1 %collective-permute-done.12 = f32[4,2,96,768]{3,2,0,1:T(8,128)} collective-permute-done((f32[4,2,96,768]{3,2,0,1:T(8,128)}, f32[4,2,96,768]{3,2,0,1:T(8,128)}, u32[]{:S(2)}, u32[]{:S(2)}) %collective-permute-start.12) | collective-permute-done | bytes 2359328 | tf_op jit(solution)/shard_map/ppermute | solution.py:37
  105.4 1.9 %maximum_add_fusion = f32[4,2,96,768]{3,2,0,1:T(8,128)S(1)} fusion(f32[4,2,96,768]{3,2,0,1:T(8,128)} %collective-permute-done.12, f32[4,2,96,384]{3,2,0,1:T(8,128)S(1)} %bitcast.54, f32[4,2,96,384]{3,2,0,1:T(8,128)S(1)} %bitcast.53), kind=kLoop, calls=%fused_computation.51 | loop fusion | flops 1179648 | bytes 7077888 | tf_op jit(solution)/shard_map/add | solution.py:63
  107.3 13.5 %collective-permute-done.11 = bf16[768,512]{1,0:T(8,128)(2,1)} collective-permute-done((bf16[768,512]{1,0:T(8,128)(2,1)}, bf16[768,512]{1,0:T(8,128)(2,1)}, u32[]{:S(2)}, u32[]{:S(2)}) %collective-permute-start.11) | collective-permute-done | bytes 786464 | tf_op jit(solution)/shard_map/ppermute | solution.py:37
  120.8 1.3 convert_element_type.187
  122.2 2.0 %fusion.48 = (bf16[768,256]{1,0:T(8,128)(2,1)S(1)}, bf16[768,256]{1,0:T(8,128)(2,1)S(1)}) fusion(f32[768,2304]{1,0:T(8,128)} %copy-done.8, f32[768,512]{1,0:T(8,128)S(1)} %convert_element_type.187, f32[768,1024]{1,0:T(8,128)} %collective-permute-done.10, pred[]{:T(512)S(6)} %eq.44, pred[]{:T(512)S(6)} %eq.45, pred[]{:T(512)S(6)} %eq.47, pred[]{:T(512)S(6)} %eq.46), kind=kLoop, calls=%fused_computation.116 | loop fusion | flops 1966080 | bytes 3932164 | tf_op jit(solution)/shard_map/convert_element_type | solution.py:364
  124.1 1.3 collective-permute-start.14
  125.4 4.6 %collective-permute-start.15 = (bf16[768,256]{1,0:T(8,128)(2,1)S(1)}, bf16[768,256]{1,0:T(8,128)(2,1)S(1)}, u32[]{:S(2)}, u32[]{:S(2)}) collective-permute-start(bf16[768,256]{1,0:T(8,128)(2,1)S(1)} %get-tuple-element.28), channel_id=1, source_target_pairs={{0,8},{2,10},{4,12},{6,14},{8,16},{10,18},{12,20},{14,22},{16,24},... | collective-permute-start | bytes 1179656 | tf_op jit(solution)/shard_map/ppermute | solution.py:43
  130.7 1.6 collective-permute-start.13
  132.3 4.3 %collective-permute-done.14 = bf16[768,256]{1,0:T(8,128)(2,1)S(1)} collective-permute-done((bf16[768,256]{1,0:T(8,128)(2,1)S(1)}, bf16[768,256]{1,0:T(8,128)(2,1)S(1)}, u32[]{:S(2)}, u32[]{:S(2)}) %collective-permute-start.14) | collective-permute-done | bytes 393248 | tf_op jit(solution)/shard_map/ppermute | solution.py:43
  136.6 1.2 collective-permute-done.15
  137.8 1.7 fusion.51
  139.5 0.9 fusion.118
  141.4 2.6 %copy.62 = f32[4,2,2,96,768]{4,3,1,0,2:T(8,128)} copy(f32[4,2,2,96,768]{4,3,2,1,0:T(8,128)S(1)} %bitcast.50) | data formatting | bytes 9437184 | tf_op jit(solution)/shard_map/reshape | solution.py:385
  145.2 30.5 %shard_map.137 = (f32[96,768]{1,0:T(8,128)S(1)}, f32[96,768]{1,0:T(8,128)S(1)}, f32[256,768]{1,0:T(8,128)S(1)}) custom-call(f32[4,96,768]{2,1,0:T(8,128)S(1)} %bitcast_add_fusion.early_ref, f32[2,4,2,96,768]{4,3,2,1,0:T(8,128)} %bitcast.49, f32[256,768]{1,0:T(8,128)S(1)} %get-tuple-element.34.kept_ref, f32[256,768]{1,0:T(8,128)S(1)} %get-tuple-element.33.sent_ref), custom_call_target="tpu_custom_call" | custom-call | tf_op jit(solution)/shard_map/pallas_call | solution.py:216
  175.7 0.9 select_convert_fusion
  (161 shorter events, 28.9 us)
Async XLA Ops:
  0.6 48.8 %copy-start = (bf16[1536,384]{1,0:T(8,128)(2,1)S(1)}, bf16[1536,384]{1,0:T(8,128)(2,1)}, u32[]{:S(2)}) copy-start(bf16[1536,384]{1,0:T(8,128)(2,1)} %param.16) | copy-start | bytes 3538948
  0.6 22.0 %copy-start.19 = (bf16[1536,384]{1,0:T(8,128)(2,1)S(1)}, bf16[1536,384]{1,0:T(8,128)(2,1)}, u32[]{:S(2)}) copy-start(bf16[1536,384]{1,0:T(8,128)(2,1)} %param.17) | copy-start | bytes 3538948
  0.7 13.2 %collective-permute-start = (bf16[256,768]{1,0:T(8,128)(2,1)}, bf16[256,768]{1,0:T(8,128)(2,1)S(1)}, u32[]{:S(2)}, u32[]{:S(2)}) collective-permute-start(bf16[256,768]{1,0:T(8,128)(2,1)} %param.10), channel_id=1, source_target_pairs={{0,1},{1,0},{2,3},{3,2},{4,5},{5,4},{6,7},{7,6},{8,9},{9,8},{10,11... | collective-permute-start | bytes 1179656 | tf_op jit(solution)/shard_map/ppermute | solution.py:37
  3.7 17.8 %collective-permute-start.9 = (bf16[256,768]{1,0:T(8,128)(2,1)}, bf16[256,768]{1,0:T(8,128)(2,1)S(1)}, u32[]{:S(2)}, u32[]{:S(2)}) collective-permute-start(bf16[256,768]{1,0:T(8,128)(2,1)} %param.11), channel_id=1, source_target_pairs={{0,1},{1,0},{2,3},{3,2},{4,5},{5,4},{6,7},{7,6},{8,9},{9,8},{10,11... | collective-permute-start | bytes 1179656 | tf_op jit(solution)/shard_map/ppermute | solution.py:37
  6.6 42.8 %copy-start.31 = (pred[256]{0:T(512)(128)(4,1)}, pred[256]{0:T(512)(128)(4,1)S(1)}, u32[]{:S(2)}) copy-start(pred[256]{0:T(512)(128)(4,1)S(1)} %compare_reduce_fusion) | copy-start | bytes 772
  22.6 26.8 %copy-start.9 = (bf16[256,768]{1,0:T(8,128)(2,1)}, bf16[256,768]{1,0:T(8,128)(2,1)S(1)}, u32[]{:S(2)}) copy-start(bf16[256,768]{1,0:T(8,128)(2,1)S(1)} %get-tuple-element.60) | copy-start | bytes 1179652
  22.6 26.8 %copy-start.12 = (bf16[256,768]{1,0:T(8,128)(2,1)}, bf16[256,768]{1,0:T(8,128)(2,1)S(1)}, u32[]{:S(2)}) copy-start(bf16[256,768]{1,0:T(8,128)(2,1)S(1)} %get-tuple-element.61) | copy-start | bytes 1179652
  22.7 28.0 %copy-start.15 = (bf16[256,768]{1,0:T(8,128)(2,1)}, bf16[256,768]{1,0:T(8,128)(2,1)S(1)}, u32[]{:S(2)}) copy-start(bf16[256,768]{1,0:T(8,128)(2,1)S(1)} %get-tuple-element.35) | copy-start | bytes 1179652
  22.7 28.0 %copy-start.17 = (bf16[256,768]{1,0:T(8,128)(2,1)}, bf16[256,768]{1,0:T(8,128)(2,1)S(1)}, u32[]{:S(2)}) copy-start(bf16[256,768]{1,0:T(8,128)(2,1)S(1)} %get-tuple-element.36) | copy-start | bytes 1179652
  22.7 1.8 %copy-start.21 = (bf16[1536,384]{1,0:T(8,128)(2,1)S(1)}, bf16[1536,384]{1,0:T(8,128)(2,1)}, u32[]{:S(2)}) copy-start(bf16[1536,384]{1,0:T(8,128)(2,1)} %param.18) | copy-start | bytes 3538948
  25.2 11.2 %collective-permute-start.1 = (bf16[256,768]{1,0:T(8,128)(2,1)S(1)}, bf16[256,768]{1,0:T(8,128)(2,1)S(1)}, u32[]{:S(2)}, u32[]{:S(2)}) collective-permute-start(bf16[256,768]{1,0:T(8,128)(2,1)S(1)} %pad_maximum_fusion.4), channel_id=1, source_target_pairs={{0,8},{2,10},{4,12},{6,14},{8,16},{10,18},{12,20},{14,22},{16,24},... | collective-permute-start | bytes 1179656 | tf_op jit(solution)/shard_map/ppermute | solution.py:43
  28.9 11.6 %collective-permute-start.2 = (bf16[256,768]{1,0:T(8,128)(2,1)S(1)}, bf16[256,768]{1,0:T(8,128)(2,1)S(1)}, u32[]{:S(2)}, u32[]{:S(2)}) collective-permute-start(bf16[256,768]{1,0:T(8,128)(2,1)S(1)} %pad_maximum_fusion.4), channel_id=1, source_target_pairs={{8,0},{10,2},{12,4},{14,6},{16,8},{18,10},{20,12},{22,14},{24,16},... | collective-permute-start | bytes 1179656 | tf_op jit(solution)/shard_map/ppermute | solution.py:43
  30.3 12.0 %collective-permute-start.5 = (bf16[256,768]{1,0:T(8,128)(2,1)S(1)}, bf16[256,768]{1,0:T(8,128)(2,1)S(1)}, u32[]{:S(2)}, u32[]{:S(2)}) collective-permute-start(bf16[256,768]{1,0:T(8,128)(2,1)S(1)} %pad_maximum_fusion.4), channel_id=1, source_target_pairs={{0,4},{2,6},{4,0},{6,2},{8,12},{10,14},{12,8},{14,10},{16,20},{18,... | collective-permute-start | bytes 1179656 | tf_op jit(solution)/shard_map/ppermute | solution.py:37
  40.6 10.1 %copy-start.34 = (bf16[384,1536]{1,0:T(8,128)(2,1)S(1)}, bf16[384,1536]{1,0:T(8,128)(2,1)}, u32[]{:S(2)}) copy-start(bf16[384,1536]{1,0:T(8,128)(2,1)} %param.19) | copy-start | bytes 3538948
  40.6 8.8 %collective-permute-start.3 = (bf16[256,768]{1,0:T(8,128)(2,1)S(1)}, bf16[256,768]{1,0:T(8,128)(2,1)S(1)}, u32[]{:S(2)}, u32[]{:S(2)}) collective-permute-start(bf16[256,768]{1,0:T(8,128)(2,1)S(1)} %get-tuple-element.38), channel_id=1, source_target_pairs={{0,4},{2,6},{4,0},{6,2},{8,12},{10,14},{12,8},{14,10},{16,20},{18,... | collective-permute-start | bytes 1179656 | tf_op jit(solution)/shard_map/ppermute | solution.py:37
  42.2 9.9 %collective-permute-start.8 = (bf16[256,768]{1,0:T(8,128)(2,1)S(1)}, bf16[256,768]{1,0:T(8,128)(2,1)S(1)}, u32[]{:S(2)}, u32[]{:S(2)}) collective-permute-start(bf16[256,768]{1,0:T(8,128)(2,1)S(1)} %pad_maximum_fusion.4), channel_id=1, source_target_pairs={{0,2},{2,0},{4,6},{6,4},{8,10},{10,8},{12,14},{14,12},{16,18},{18,... | collective-permute-start | bytes 1179656 | tf_op jit(solution)/shard_map/ppermute | solution.py:37
  42.3 9.0 %collective-permute-start.6 = (bf16[256,768]{1,0:T(8,128)(2,1)S(1)}, bf16[256,768]{1,0:T(8,128)(2,1)S(1)}, u32[]{:S(2)}, u32[]{:S(2)}) collective-permute-start(bf16[256,768]{1,0:T(8,128)(2,1)S(1)} %collective-permute-done.5), channel_id=1, source_target_pairs={{0,2},{2,0},{4,6},{6,4},{8,10},{10,8},{12,14},{14,12},{16,18},{18,... | collective-permute-start | bytes 1179656 | tf_op jit(solution)/shard_map/ppermute | solution.py:37
  49.5 1.8 %collective-permute-start.4 = (bf16[256,768]{1,0:T(8,128)(2,1)S(1)}, bf16[256,768]{1,0:T(8,128)(2,1)S(1)}, u32[]{:S(2)}, u32[]{:S(2)}) collective-permute-start(bf16[256,768]{1,0:T(8,128)(2,1)S(1)} %collective-permute-done.3), channel_id=1, source_target_pairs={{0,2},{2,0},{4,6},{6,4},{8,10},{10,8},{12,14},{14,12},{16,18},{18,... | collective-permute-start | bytes 1179656 | tf_op jit(solution)/shard_map/ppermute | solution.py:37
  50.1 1.9 %collective-permute-start.7 = (bf16[256,768]{1,0:T(8,128)(2,1)S(1)}, bf16[256,768]{1,0:T(8,128)(2,1)S(1)}, u32[]{:S(2)}, u32[]{:S(2)}) collective-permute-start(bf16[256,768]{1,0:T(8,128)(2,1)S(1)} %get-tuple-element.37), channel_id=1, source_target_pairs={{0,2},{2,0},{4,6},{6,4},{8,10},{10,8},{12,14},{14,12},{16,18},{18,... | collective-permute-start | bytes 1179656 | tf_op jit(solution)/shard_map/ppermute | solution.py:37
  52.3 18.5 %copy-start.1 = (bf16[2304,768]{1,0:T(8,128)(2,1)}, bf16[2304,768]{1,0:T(8,128)(2,1)S(1)}, u32[]{:S(2)}) copy-start(bf16[2304,768]{1,0:T(8,128)(2,1)S(1)} %constant_dynamic-update-slice_fusion.1) | copy-start | bytes 10616836
  61.2 4.7 %copy-start.26 = (bf16[256,64]{1,0:T(8,128)(2,1)}, bf16[256,64]{1,0:T(8,128)(2,1)S(1)}, u32[]{:S(2)}) copy-start(bf16[256,64]{1,0:T(8,128)(2,1)S(1)} %convolution_convert_fusion.5) | copy-start | bytes 98308
  62.4 3.5 %copy-start.27 = (bf16[256,64]{1,0:T(8,128)(2,1)}, bf16[256,64]{1,0:T(8,128)(2,1)S(1)}, u32[]{:S(2)}) copy-start(bf16[256,64]{1,0:T(8,128)(2,1)S(1)} %convolution_convert_fusion.6) | copy-start | bytes 98308
  63.7 2.3 %copy-start.28 = (bf16[256,64]{1,0:T(8,128)(2,1)}, bf16[256,64]{1,0:T(8,128)(2,1)S(1)}, u32[]{:S(2)}) copy-start(bf16[256,64]{1,0:T(8,128)(2,1)S(1)} %convolution_convert_fusion.7) | copy-start | bytes 98308
  66.0 1.5 copy-start.30
  68.0 3.6 %copy-start.6 = (bf16[256,2304]{1,0:T(8,128)(2,1)}, bf16[256,2304]{1,0:T(8,128)(2,1)S(1)}, u32[]{:S(2)}) copy-start(bf16[256,2304]{1,0:T(8,128)(2,1)S(1)} %fusion.12) | copy-start | bytes 3538948
  68.8 3.2 %copy-start.7 = (bf16[256,2304]{1,0:T(8,128)(2,1)}, bf16[256,2304]{1,0:T(8,128)(2,1)S(1)}, u32[]{:S(2)}) copy-start(bf16[256,2304]{1,0:T(8,128)(2,1)S(1)} %fusion.13) | copy-start | bytes 3538948
  69.4 3.0 %copy-start.5 = (bf16[256,2304]{1,0:T(8,128)(2,1)}, bf16[256,2304]{1,0:T(8,128)(2,1)S(1)}, u32[]{:S(2)}) copy-start(bf16[256,2304]{1,0:T(8,128)(2,1)S(1)} %fusion.14) | copy-start | bytes 3538948
  70.2 2.6 %copy-start.3 = (bf16[256,2304]{1,0:T(8,128)(2,1)}, bf16[256,2304]{1,0:T(8,128)(2,1)S(1)}, u32[]{:S(2)}) copy-start(bf16[256,2304]{1,0:T(8,128)(2,1)S(1)} %fusion.15) | copy-start | bytes 3538948
  77.3 2.9 %copy-start.8 = (f32[768,2304]{1,0:T(8,128)}, f32[768,2304]{1,0:T(8,128)S(1)}, u32[]{:S(2)}) copy-start(f32[768,2304]{1,0:T(8,128)S(1)} %convolution_dynamic-update-slice_fusion) | copy-start | bytes 21233668
  82.3 10.6 %collective-permute-start.10 = (f32[768,1024]{1,0:T(8,128)}, f32[768,1024]{1,0:T(8,128)}, u32[]{:S(2)}, u32[]{:S(2)}) collective-permute-start(f32[768,1024]{1,0:T(8,128)} %slice.206), channel_id=1, source_target_pairs={{0,2},{2,0},{4,6},{6,4},{8,10},{10,8},{12,14},{14,12},{16,18},{18,... | collective-permute-start | bytes 9437192 | tf_op jit(solution)/shard_map/ppermute | solution.py:37
  84.4 4.3 %copy-start.2 = (bf16[2304,768]{1,0:T(8,128)(2,1)S(1)}, bf16[2304,768]{1,0:T(8,128)(2,1)}, u32[]{:S(2)}) copy-start(bf16[2304,768]{1,0:T(8,128)(2,1)} %copy-done.1) | copy-start | bytes 10616836
  84.4 6.1 %copy-start.4 = (bf16[256,2304]{1,0:T(8,128)(2,1)S(1)}, bf16[256,2304]{1,0:T(8,128)(2,1)}, u32[]{:S(2)}) copy-start(bf16[256,2304]{1,0:T(8,128)(2,1)} %copy-done.3) | copy-start | bytes 3538948
  92.8 3.9 %copy-start.23 = (bf16[256,384]{0,1:T(8,128)(2,1)}, bf16[256,384]{0,1:T(8,128)(2,1)S(1)}, u32[]{:S(2)}) copy-start(bf16[256,384]{0,1:T(8,128)(2,1)S(1)} %fusion.44) | copy-start | bytes 589828
  92.8 3.2 %copy-start.10 = (bf16[256,768]{1,0:T(8,128)(2,1)S(1)}, bf16[256,768]{1,0:T(8,128)(2,1)}, u32[]{:S(2)}) copy-start(bf16[256,768]{1,0:T(8,128)(2,1)} %copy-done.9) | copy-start | bytes 1179652
  92.8 3.1 %copy-start.13 = (bf16[256,768]{1,0:T(8,128)(2,1)S(1)}, bf16[256,768]{1,0:T(8,128)(2,1)}, u32[]{:S(2)}) copy-start(bf16[256,768]{1,0:T(8,128)(2,1)} %copy-done.12) | copy-start | bytes 1179652
  92.9 3.1 %copy-start.32 = (pred[256]{0:T(512)(128)(4,1)S(1)}, pred[256]{0:T(512)(128)(4,1)}, u32[]{:S(2)}) copy-start(pred[256]{0:T(512)(128)(4,1)} %copy-done.31) | copy-start | bytes 772
  96.9 1.1 copy-start.25
  100.6 4.9 %collective-permute-start.12 = (f32[4,2,96,768]{3,2,0,1:T(8,128)}, f32[4,2,96,768]{3,2,0,1:T(8,128)}, u32[]{:S(2)}, u32[]{:S(2)}) collective-permute-start(f32[4,2,96,768]{3,2,0,1:T(8,128)} %pad_maximum_fusion), channel_id=1, source_target_pairs={{0,2},{2,0},{4,6},{6,4},{8,10},{10,8},{12,14},{14,12},{16,18},{18,... | collective-permute-start | bytes 7077896 | tf_op jit(solution)/shard_map/ppermute | solution.py:37
  100.7 20.1 %collective-permute-start.11 = (bf16[768,512]{1,0:T(8,128)(2,1)}, bf16[768,512]{1,0:T(8,128)(2,1)}, u32[]{:S(2)}, u32[]{:S(2)}) collective-permute-start(bf16[768,512]{1,0:T(8,128)(2,1)} %fusion.32), channel_id=1, source_target_pairs={{0,4},{2,6},{4,0},{6,2},{8,12},{10,14},{12,8},{14,10},{16,20},{18,... | collective-permute-start | bytes 2359304 | tf_op jit(solution)/shard_map/ppermute | solution.py:37
  122.2 7.8 %copy-start.24 = (bf16[256,384]{0,1:T(8,128)(2,1)S(1)}, bf16[256,384]{0,1:T(8,128)(2,1)}, u32[]{:S(2)}) copy-start(bf16[256,384]{0,1:T(8,128)(2,1)} %copy-done.23) | copy-start | bytes 589828
  124.1 12.5 %collective-permute-start.14 = (bf16[768,256]{1,0:T(8,128)(2,1)S(1)}, bf16[768,256]{1,0:T(8,128)(2,1)S(1)}, u32[]{:S(2)}, u32[]{:S(2)}) collective-permute-start(bf16[768,256]{1,0:T(8,128)(2,1)S(1)} %get-tuple-element.27), channel_id=1, source_target_pairs={{8,0},{10,2},{12,4},{14,6},{16,8},{18,10},{20,12},{22,14},{24,16},... | collective-permute-start | bytes 1179656 | tf_op jit(solution)/shard_map/ppermute | solution.py:43
  125.4 12.4 %collective-permute-start.15 = (bf16[768,256]{1,0:T(8,128)(2,1)S(1)}, bf16[768,256]{1,0:T(8,128)(2,1)S(1)}, u32[]{:S(2)}, u32[]{:S(2)}) collective-permute-start(bf16[768,256]{1,0:T(8,128)(2,1)S(1)} %get-tuple-element.28), channel_id=1, source_target_pairs={{0,8},{2,10},{4,12},{6,14},{8,16},{10,18},{12,20},{14,22},{16,24},... | collective-permute-start | bytes 1179656 | tf_op jit(solution)/shard_map/ppermute | solution.py:43
  130.6 8.8 %copy-start.11 = (bf16[256,768]{1,0:T(8,128)(2,1)S(1)}, bf16[256,768]{1,0:T(8,128)(2,1)}, u32[]{:S(2)}) copy-start(bf16[256,768]{1,0:T(8,128)(2,1)} %copy-done.9) | copy-start | bytes 1179652
  130.6 8.8 %copy-start.14 = (bf16[256,768]{1,0:T(8,128)(2,1)S(1)}, bf16[256,768]{1,0:T(8,128)(2,1)}, u32[]{:S(2)}) copy-start(bf16[256,768]{1,0:T(8,128)(2,1)} %copy-done.12) | copy-start | bytes 1179652
  130.7 8.8 %copy-start.33 = (pred[256]{0:T(512)(128)(4,1)S(1)}, pred[256]{0:T(512)(128)(4,1)}, u32[]{:S(2)}) copy-start(pred[256]{0:T(512)(128)(4,1)} %copy-done.31) | copy-start | bytes 772
  130.7 14.3 %collective-permute-start.13 = (bf16[4,96,768]{2,1,0:T(8,128)(2,1)S(1)}, bf16[4,96,768]{2,1,0:T(8,128)(2,1)S(1)}, u32[]{:S(2)}, u32[]{:S(2)}) collective-permute-start(bf16[4,96,768]{2,1,0:T(8,128)(2,1)S(1)} %fusion.52), channel_id=1, source_target_pairs={{0,4},{2,6},{4,0},{6,2},{8,12},{10,14},{12,8},{14,10},{16,20},{18,... | collective-permute-start | bytes 1769480 | tf_op jit(solution)/shard_map/ppermute | solution.py:37
  139.5 1.3 copy-start.20
  141.4 2.6 %copy-start.22 = (bf16[1536,384]{1,0:T(8,128)(2,1)S(1)}, bf16[1536,384]{1,0:T(8,128)(2,1)}, u32[]{:S(2)}) copy-start(bf16[1536,384]{1,0:T(8,128)(2,1)} %param.18) | copy-start | bytes 3538948
  (3 other events, 3.2 us)
